TPU v7x, 512 devices: a whole 4x4x16 slice. The times are simulated.
512 devices in a mesh: seq: 64 (over z, y_lo, core), mp: 8 (over y_hi, x).
Axes of the slice: x: 4, y: 4 (y_hi: 2, y_lo: 2; y = y_hi * 2 + y_lo), z: 16, core: 2. Of those that a mesh axis runs over, the one named last changes fastest.
Arguments:
- layer_input: bfloat16 [16384, 8192], P('seq', 'mp'), may hold values from -8 to 8
- query_heads: bfloat16 [16384, 1024], P('seq', 'mp'), may hold values from -100 to 100
- key_head: bfloat16 [16384, 128], P('seq'), may hold values from -5 to 5
- value_head: bfloat16 [16384, 128], P('seq'), may hold values from -6 to 6
- attn_grad: bfloat16 [16384, 1024], P('seq', 'mp'), may hold values from -6 to 6
- block_order: int32 [128], replicated, may hold values from 0 to 127, as said below
- owners: int32 [8, 64], P('mp'), may hold values from 0 to 63, each once within a row
Outputs:
- query_grad: bfloat16 [16384, 1024], P('seq', 'mp')
- grad_blocks: float32 [8, 64, 64, 64], P('mp', 'seq')
- left_stats: float32 [8, 64, 64, 64], P('mp', 'seq')
- right_stats: float32 [8, 64, 64, 64], P('mp', 'seq')
Inputs may be any that keep to these rules, and one draw needn't show every extreme that they name: `block_order`: storage block 2 s + 1 holds position block 127 minus the position block of storage block 2 s; the position blocks of storage blocks 0, 2, 4, ... run cyclically through 0 to 63, upward or downward, from a drawn start. `owners`: each row is a permutation.
All inputs are finite; a program needn't handle non-finite values.
Results may differ from a plain program's by a relative error of at most 0.009.
Values may be sent and summed in bfloat16 or wider, within the bound.
A program may use at most 64 MiB of HBM per device.

v0:
```python
import math

import jax
import jax.numpy as jnp
from jax import lax
from jax.sharding import PartitionSpec as P

W = 2
BLK = 64


MASKED = -1e30


def passed_along(block, axis, distance):
    devices = range(lax.axis_size(axis))
    route = [((i - distance) % len(devices), i) for i in devices]
    return lax.ppermute(block, axis, route)


def shards(layer_input, query_heads, key_head, value_head, attn_grad, block_order, owners):
    row_count = key_head.shape[0]
    half_rows = row_count // 2
    head_width = key_head.shape[1]
    heads_here = query_heads.shape[1] // head_width
    score_scale = 1.0 / math.sqrt(head_width)
    reach_span = W * half_rows
    cycle_size = lax.axis_size("seq")
    cycle_place = lax.axis_index("seq")
    queries = query_heads.reshape(2, half_rows, heads_here, head_width)
    grads_out = attn_grad.reshape(2, half_rows, heads_here, head_width)

    def blocks_of(device):
        return lax.dynamic_slice(block_order, (2 * device,), (2,))

    own_blocks = blocks_of(cycle_place)
    offsets = [0] + [step for step in range(1, W + 1)] + [-step for step in range(1, W + 1)]
    sources = []
    for offset in offsets:
        anchor = (cycle_place - offset) % cycle_size
        their_blocks = blocks_of(anchor)
        if offset == 0:
            keys_here, values_here = (key_head, value_head)
        else:
            keys_here, values_here = passed_along((key_head, value_head), "seq", offset)
        sources.append(
            (
                keys_here.reshape(2, half_rows, head_width),
                values_here.reshape(2, half_rows, head_width),
                their_blocks,
            )
        )
    in_block = jnp.arange(half_rows, dtype=jnp.int32)

    def visible_mask(q_block, k_block):
        apart = (q_block - k_block) * half_rows + in_block[:, None] - in_block[None, :]
        return (apart >= 0) & (apart < reach_span)

    def tile_scores(q_slot, keys_blk, tile_mask):
        raw_scores = (
            jnp.einsum("qhd,kd->hqk", queries[q_slot], keys_blk, preferred_element_type=jnp.float32)
            * score_scale
        )
        return jnp.where(tile_mask[None], raw_scores, MASKED)

    maxima = [jnp.full((heads_here, half_rows), MASKED, jnp.float32) for q_slot in range(2)]
    totals = [jnp.zeros((heads_here, half_rows), jnp.float32) for q_slot in range(2)]
    for keys_src, values_src, their_blocks in sources:
        for q_slot in range(2):
            for k_slot in range(2):
                tile_mask = visible_mask(own_blocks[q_slot], their_blocks[k_slot])

                def update(
                    q_slot=q_slot,
                    keys_blk=keys_src[k_slot],
                    tile_mask=tile_mask,
                    run_max=maxima[q_slot],
                    run_sum=totals[q_slot],
                ):
                    scores = tile_scores(q_slot, keys_blk, tile_mask)
                    new_max = jnp.maximum(run_max, jnp.max(scores, -1))
                    new_sum = run_sum * jnp.exp(run_max - new_max) + jnp.sum(
                        jnp.exp(scores - new_max[..., None]), -1
                    )
                    return (new_max, new_sum)

                maxima[q_slot], totals[q_slot] = update()
    log_totals = [maxima[q_slot] + jnp.log(totals[q_slot]) for q_slot in range(2)]
    attended = [jnp.zeros((half_rows, heads_here, head_width), jnp.float32) for q_slot in range(2)]
    for keys_src, values_src, their_blocks in sources:
        for q_slot in range(2):
            for k_slot in range(2):
                tile_mask = visible_mask(own_blocks[q_slot], their_blocks[k_slot])

                def forward(
                    q_slot=q_slot,
                    keys_blk=keys_src[k_slot],
                    values_blk=values_src[k_slot],
                    tile_mask=tile_mask,
                    running=attended[q_slot],
                ):
                    prob = jnp.exp(
                        tile_scores(q_slot, keys_blk, tile_mask) - log_totals[q_slot][..., None]
                    )
                    prob_b = prob.astype(jnp.bfloat16)
                    return running + jnp.einsum(
                        "hqk,kd->qhd", prob_b, values_blk, preferred_element_type=jnp.float32
                    )

                attended[q_slot] = forward()
    delta_rows = [
        jnp.sum(grads_out[q_slot].astype(jnp.float32) * attended[q_slot], -1).T
        for q_slot in range(2)
    ]
    query_acc = [jnp.zeros((half_rows, heads_here, head_width), jnp.float32) for q_slot in range(2)]
    running = jnp.zeros((2, half_rows, 2 * head_width), jnp.float32)
    for offset, (keys_src, values_src, their_blocks) in zip(offsets, sources):
        key_grads = [jnp.zeros((half_rows, head_width), jnp.float32) for k_slot in range(2)]
        value_grads = [jnp.zeros((half_rows, head_width), jnp.float32) for k_slot in range(2)]
        for q_slot in range(2):
            for k_slot in range(2):
                tile_mask = visible_mask(own_blocks[q_slot], their_blocks[k_slot])
                carried = (query_acc[q_slot], key_grads[k_slot], value_grads[k_slot])

                def backward(
                    q_slot=q_slot,
                    keys_blk=keys_src[k_slot],
                    values_blk=values_src[k_slot],
                    tile_mask=tile_mask,
                    carried=carried,
                ):
                    prob = jnp.exp(
                        tile_scores(q_slot, keys_blk, tile_mask) - log_totals[q_slot][..., None]
                    )
                    prob_b = prob.astype(jnp.bfloat16)
                    dprob = jnp.einsum(
                        "qhd,kd->hqk",
                        grads_out[q_slot],
                        values_blk,
                        preferred_element_type=jnp.float32,
                    )
                    dscore = (prob * (dprob - delta_rows[q_slot][..., None])).astype(jnp.bfloat16)
                    query_new = carried[0] + jnp.einsum(
                        "hqk,kd->qhd", dscore, keys_blk, preferred_element_type=jnp.float32
                    )
                    key_new = carried[1] + jnp.einsum(
                        "hqk,qhd->kd", dscore, queries[q_slot], preferred_element_type=jnp.float32
                    )
                    value_new = carried[2] + jnp.einsum(
                        "hqk,qhd->kd", prob_b, grads_out[q_slot], preferred_element_type=jnp.float32
                    )
                    return (query_new, key_new, value_new)

                query_acc[q_slot], key_grads[k_slot], value_grads[k_slot] = backward()
        head_part = jnp.concatenate(
            [jnp.concatenate(key_grads, 0) * score_scale, jnp.concatenate(value_grads, 0)], 1
        )
        paired = head_part.reshape(2, half_rows, 2 * head_width)
        if offset != 0:
            paired = passed_along(paired, "seq", -offset)
        running = running + paired
    kv_grad = lax.psum(running, "mp").astype(jnp.bfloat16).reshape(row_count, 2 * head_width)
    query_out = (
        (jnp.stack(query_acc, 0) * score_scale)
        .reshape(row_count, heads_here * head_width)
        .astype(jnp.bfloat16)
    )
    weight_part = jnp.einsum(
        "rd,rc->dc", layer_input, kv_grad, preferred_element_type=jnp.float32
    ) * (1.0 / math.sqrt(row_count * cycle_size))
    row_blocks = weight_part.shape[0] // BLK
    column_blocks = weight_part.shape[1] // BLK
    pieces = (
        weight_part.reshape(row_blocks, BLK, column_blocks, BLK)
        .transpose(0, 2, 1, 3)
        .reshape(row_blocks * column_blocks, BLK, BLK)
    )
    arranged = jnp.zeros_like(pieces).at[owners[0]].set(pieces)
    owned = lax.psum_scatter(arranged, "seq", scatter_dimension=0, tiled=True)
    left_stats = jnp.einsum("bij,bkj->bik", owned, owned, precision=lax.Precision.HIGHEST) / BLK
    right_stats = jnp.einsum("bji,bjk->bik", owned, owned, precision=lax.Precision.HIGHEST) / BLK
    return (query_out, owned[None], left_stats[None], right_stats[None])


def solution(mesh):
    return jax.shard_map(
        shards,
        mesh=mesh,
        in_specs=(
            P("seq", "mp"),
            P("seq", "mp"),
            P("seq", None),
            P("seq", None),
            P("seq", "mp"),
            P(),
            P("mp", None),
        ),
        out_specs=(
            P("seq", "mp"),
            P("mp", "seq", None, None),
            P("mp", "seq", None, None),
            P("mp", "seq", None, None),
        ),
        check_vma=False,
    )
```

profile of v0, /device:TPU:1, one launch (start us, length us, event | category | flops | bytes accessed | tf_op | source)
XLA Modules:
  0.0 403.0 jit_solution(184374108674276057)
XLA Ops:
  7.3 4.2 %collective-permute-start.1 = (bf16[256,128]{1,0:T(8,128)(2,1)}, bf16[256,128]{1,0:T(8,128)(2,1)S(1)}, u32[]{:S(2)}, u32[]{:S(2)}) collective-permute-start(bf16[256,128]{1,0:T(8,128)(2,1)} %param.9), channel_id=1, source_target_pairs={{496,0},{504,8},{0,16},{8,24},{16,32},{24,40},{32,48},{40,56},{48,... | collective-permute-start | bytes 196616 | tf_op jit(solution)/shard_map/ppermute | solution.py:18
  11.4 4.3 %collective-permute-start = (bf16[256,128]{1,0:T(8,128)(2,1)}, bf16[256,128]{1,0:T(8,128)(2,1)S(1)}, u32[]{:S(2)}, u32[]{:S(2)}) collective-permute-start(bf16[256,128]{1,0:T(8,128)(2,1)} %param.9), channel_id=1, source_target_pairs={{504,0},{0,8},{8,16},{16,24},{24,32},{32,40},{40,48},{48,56},{56,6... | collective-permute-start | bytes 196616 | tf_op jit(solution)/shard_map/ppermute | solution.py:18
  15.7 8.5 %collective-permute-start.3 = (bf16[256,128]{1,0:T(8,128)(2,1)}, bf16[256,128]{1,0:T(8,128)(2,1)S(1)}, u32[]{:S(2)}, u32[]{:S(2)}) collective-permute-start(bf16[256,128]{1,0:T(8,128)(2,1)} %param.9), channel_id=1, source_target_pairs={{16,0},{24,8},{32,16},{40,24},{48,32},{56,40},{64,48},{72,56},{80,... | collective-permute-start | bytes 196616 | tf_op jit(solution)/shard_map/ppermute | solution.py:18
  24.2 2.9 collective-permute-start.2
  27.1 1.9 collective-permute-start.5
  29.1 1.0 fusion.547
  63.5 2.7 collective-permute-start.4
  68.1 6.0 %collective-permute-start.7 = (bf16[256,128]{1,0:T(8,128)(2,1)}, bf16[256,128]{1,0:T(8,128)(2,1)S(1)}, u32[]{:S(2)}, u32[]{:S(2)}) collective-permute-start(bf16[256,128]{1,0:T(8,128)(2,1)} %param.10), channel_id=1, source_target_pairs={{16,0},{24,8},{32,16},{40,24},{48,32},{56,40},{64,48},{72,56},{80,... | collective-permute-start | bytes 196616 | tf_op jit(solution)/shard_map/ppermute | solution.py:18
  76.1 2.6 collective-permute-start.6
  93.5 3.4 collective-permute-start.8
  97.5 3.3 collective-permute-start.9
  101.5 2.1 collective-permute-start.10
  104.3 3.2 collective-permute-start.11
  110.4 5.8 %collective-permute-done.11 = f32[2,128,256]{2,1,0:T(8,128)S(1)} collective-permute-done((f32[2,128,256]{2,1,0:T(8,128)S(1)}, f32[2,128,256]{2,1,0:T(8,128)S(1)}, u32[]{:S(2)}, u32[]{:S(2)}) %collective-permute-start.11) | collective-permute-done | bytes 262176 | tf_op jit(solution)/shard_map/ppermute | solution.py:18
  116.3 37.5 %all-reduce.1 = bf16[2,128,256]{2,1,0:T(8,128)(2,1)S(1)} all-reduce(f32[2,128,256]{2,1,0:T(8,128)S(1)} %fusion.181), channel_id=1, replica_groups=mesh['seq'=64,'mp'=8] {'mp'}, use_global_device_ids=true, to_apply=%region_42.43 | all-reduce | flops 65536 | bytes 393216 | tf_op jit(solution)/shard_map/psum | solution.py:162
  153.8 1.3 fusion
  155.1 1.7 reshape.2370
  156.8 1.9 copy.13
  159.0 6.6 %scatter_fusion = f32[64,64,64]{2,1,0:T(8,128)S(1)} fusion(f32[64,64,64]{2,1,0:T(8,128)S(1)} %broadcast_in_dim.72, s32[64]{0:T(128)S(1)} %fusion.447, f32[64,64,64]{2,1,0:T(8,128)} %bitcast.777), kind=kCustom, calls=%fused_computation | custom fusion | bytes 3145984 | tf_op jit(solution)/shard_map/scatter | solution.py:178
  165.7 1.3 copy-done.2
  175.5 1.0 fusion.42
  177.1 215.7 %reduce-scatter.2.cloned.1.call-done = f32[1,64,64]{2,1,0:T(8,128)} async-done(((f32[64,64,64]{2,1,0:T(8,128)}), f32[1,64,64]{2,1,0:T(8,128)}) %reduce-scatter.2.cloned.1.call-update) | async-done | bytes 16400 | tf_op jit(solution)/shard_map/reduce_scatter | solution.py:179
  392.8 1.7 fusion.177
  394.5 1.6 fusion.178
  (221 shorter events, 40.0 us)
Async XLA Ops:
  7.2 146.7 %copy-start = (bf16[256,1024]{1,0:T(8,128)(2,1)S(1)}, bf16[256,1024]{1,0:T(8,128)(2,1)}, u32[]{:S(2)}) copy-start(bf16[256,1024]{1,0:T(8,128)(2,1)} %param.7) | copy-start | bytes 1572868
  7.2 68.9 %copy-start.4 = (bf16[256,128]{1,0:T(8,128)(2,1)S(1)}, bf16[256,128]{1,0:T(8,128)(2,1)}, u32[]{:S(2)}) copy-start(bf16[256,128]{1,0:T(8,128)(2,1)} %param.10) | copy-start | bytes 196612
  7.2 71.5 %copy-start.3 = (bf16[256,128]{1,0:T(8,128)(2,1)S(1)}, bf16[256,128]{1,0:T(8,128)(2,1)}, u32[]{:S(2)}) copy-start(bf16[256,128]{1,0:T(8,128)(2,1)} %param.8) | copy-start | bytes 196612
  7.2 72.7 %copy-start.1 = (bf16[256,128]{1,0:T(8,128)(2,1)S(1)}, bf16[256,128]{1,0:T(8,128)(2,1)}, u32[]{:S(2)}) copy-start(bf16[256,128]{1,0:T(8,128)(2,1)} %param.11) | copy-start | bytes 196612
  7.2 385.6 %reduce-scatter.2.cloned.1.call-start = ((), (), s32[]{:S(2)}) async-start(), calls=%async_computation.1 | async-start | bytes 2129920 | tf_op jit(solution)/shard_map/reduce_scatter | solution.py:179
  7.3 56.2 %collective-permute-start.1 = (bf16[256,128]{1,0:T(8,128)(2,1)}, bf16[256,128]{1,0:T(8,128)(2,1)S(1)}, u32[]{:S(2)}, u32[]{:S(2)}) collective-permute-start(bf16[256,128]{1,0:T(8,128)(2,1)} %param.9), channel_id=1, source_target_pairs={{496,0},{504,8},{0,16},{8,24},{16,32},{24,40},{32,48},{40,56},{48,... | collective-permute-start | bytes 196616 | tf_op jit(solution)/shard_map/ppermute | solution.py:18
  11.4 56.7 %collective-permute-start = (bf16[256,128]{1,0:T(8,128)(2,1)}, bf16[256,128]{1,0:T(8,128)(2,1)S(1)}, u32[]{:S(2)}, u32[]{:S(2)}) collective-permute-start(bf16[256,128]{1,0:T(8,128)(2,1)} %param.9), channel_id=1, source_target_pairs={{504,0},{0,8},{8,16},{16,24},{24,32},{32,40},{40,48},{48,56},{56,6... | collective-permute-start | bytes 196616 | tf_op jit(solution)/shard_map/ppermute | solution.py:18
  15.7 60.3 %collective-permute-start.3 = (bf16[256,128]{1,0:T(8,128)(2,1)}, bf16[256,128]{1,0:T(8,128)(2,1)S(1)}, u32[]{:S(2)}, u32[]{:S(2)}) collective-permute-start(bf16[256,128]{1,0:T(8,128)(2,1)} %param.9), channel_id=1, source_target_pairs={{16,0},{24,8},{32,16},{40,24},{48,32},{56,40},{64,48},{72,56},{80,... | collective-permute-start | bytes 196616 | tf_op jit(solution)/shard_map/ppermute | solution.py:18
  24.2 54.8 %collective-permute-start.2 = (bf16[256,128]{1,0:T(8,128)(2,1)}, bf16[256,128]{1,0:T(8,128)(2,1)S(1)}, u32[]{:S(2)}, u32[]{:S(2)}) collective-permute-start(bf16[256,128]{1,0:T(8,128)(2,1)} %param.9), channel_id=1, source_target_pairs={{8,0},{16,8},{24,16},{32,24},{40,32},{48,40},{56,48},{64,56},{72,6... | collective-permute-start | bytes 196616 | tf_op jit(solution)/shard_map/ppermute | solution.py:18
  27.1 56.7 %collective-permute-start.5 = (bf16[256,128]{1,0:T(8,128)(2,1)}, bf16[256,128]{1,0:T(8,128)(2,1)S(1)}, u32[]{:S(2)}, u32[]{:S(2)}) collective-permute-start(bf16[256,128]{1,0:T(8,128)(2,1)} %param.10), channel_id=1, source_target_pairs={{496,0},{504,8},{0,16},{8,24},{16,32},{24,40},{32,48},{40,56},{48,... | collective-permute-start | bytes 196616 | tf_op jit(solution)/shard_map/ppermute | solution.py:18
  63.5 45.1 %copy-start.8 = (bf16[256,128]{1,0:T(8,128)(2,1)}, bf16[256,128]{1,0:T(8,128)(2,1)S(1)}, u32[]{:S(2)}) copy-start(bf16[256,128]{1,0:T(8,128)(2,1)S(1)} %collective-permute-done.1) | copy-start | bytes 196612
  63.5 21.6 %collective-permute-start.4 = (bf16[256,128]{1,0:T(8,128)(2,1)}, bf16[256,128]{1,0:T(8,128)(2,1)S(1)}, u32[]{:S(2)}, u32[]{:S(2)}) collective-permute-start(bf16[256,128]{1,0:T(8,128)(2,1)} %param.10), channel_id=1, source_target_pairs={{504,0},{0,8},{8,16},{16,24},{24,32},{32,40},{40,48},{48,56},{56,6... | collective-permute-start | bytes 196616 | tf_op jit(solution)/shard_map/ppermute | solution.py:18
  68.1 41.4 %copy-start.6 = (bf16[256,128]{1,0:T(8,128)(2,1)}, bf16[256,128]{1,0:T(8,128)(2,1)S(1)}, u32[]{:S(2)}) copy-start(bf16[256,128]{1,0:T(8,128)(2,1)S(1)} %collective-permute-done) | copy-start | bytes 196612
  68.1 16.2 %collective-permute-start.7 = (bf16[256,128]{1,0:T(8,128)(2,1)}, bf16[256,128]{1,0:T(8,128)(2,1)S(1)}, u32[]{:S(2)}, u32[]{:S(2)}) collective-permute-start(bf16[256,128]{1,0:T(8,128)(2,1)} %param.10), channel_id=1, source_target_pairs={{16,0},{24,8},{32,16},{40,24},{48,32},{56,40},{64,48},{72,56},{80,... | collective-permute-start | bytes 196616 | tf_op jit(solution)/shard_map/ppermute | solution.py:18
  76.0 31.8 %copy-start.10 = (bf16[256,128]{1,0:T(8,128)(2,1)}, bf16[256,128]{1,0:T(8,128)(2,1)S(1)}, u32[]{:S(2)}) copy-start(bf16[256,128]{1,0:T(8,128)(2,1)S(1)} %collective-permute-done.3) | copy-start | bytes 196612
  76.1 8.6 %collective-permute-start.6 = (bf16[256,128]{1,0:T(8,128)(2,1)S(1)}, bf16[256,128]{1,0:T(8,128)(2,1)S(1)}, u32[]{:S(2)}, u32[]{:S(2)}) collective-permute-start(bf16[256,128]{1,0:T(8,128)(2,1)S(1)} %copy-done.4), channel_id=1, source_target_pairs={{8,0},{16,8},{24,16},{32,24},{40,32},{48,40},{56,48},{64,56},{72,6... | collective-permute-start | bytes 196616 | tf_op jit(solution)/shard_map/ppermute | solution.py:18
  79.0 29.2 %copy-start.9 = (bf16[256,128]{1,0:T(8,128)(2,1)}, bf16[256,128]{1,0:T(8,128)(2,1)S(1)}, u32[]{:S(2)}) copy-start(bf16[256,128]{1,0:T(8,128)(2,1)S(1)} %collective-permute-done.2) | copy-start | bytes 196612
  84.5 3.9 copy-start.7
  93.5 16.4 %collective-permute-start.8 = (f32[2,128,256]{2,1,0:T(8,128)S(1)}, f32[2,128,256]{2,1,0:T(8,128)S(1)}, u32[]{:S(2)}, u32[]{:S(2)}) collective-permute-start(f32[2,128,256]{2,1,0:T(8,128)S(1)} %pad_maximum_fusion), channel_id=1, source_target_pairs={{8,0},{16,8},{24,16},{32,24},{40,32},{48,40},{56,48},{64,56},{72,6... | collective-permute-start | bytes 786440 | tf_op jit(solution)/shard_map/ppermute | solution.py:18
  97.5 12.4 %collective-permute-start.9 = (f32[2,128,256]{2,1,0:T(8,128)S(1)}, f32[2,128,256]{2,1,0:T(8,128)S(1)}, u32[]{:S(2)}, u32[]{:S(2)}) collective-permute-start(f32[2,128,256]{2,1,0:T(8,128)S(1)} %pad_maximum_fusion.1), channel_id=1, source_target_pairs={{16,0},{24,8},{32,16},{40,24},{48,32},{56,40},{64,48},{72,56},{80,... | collective-permute-start | bytes 786440 | tf_op jit(solution)/shard_map/ppermute | solution.py:18
  101.5 8.8 %collective-permute-start.10 = (f32[2,128,256]{2,1,0:T(8,128)S(1)}, f32[2,128,256]{2,1,0:T(8,128)S(1)}, u32[]{:S(2)}, u32[]{:S(2)}) collective-permute-start(f32[2,128,256]{2,1,0:T(8,128)S(1)} %pad_maximum_fusion.2), channel_id=1, source_target_pairs={{504,0},{0,8},{8,16},{16,24},{24,32},{32,40},{40,48},{48,56},{56,6... | collective-permute-start | bytes 786440 | tf_op jit(solution)/shard_map/ppermute | solution.py:18
  104.3 11.9 %collective-permute-start.11 = (f32[2,128,256]{2,1,0:T(8,128)S(1)}, f32[2,128,256]{2,1,0:T(8,128)S(1)}, u32[]{:S(2)}, u32[]{:S(2)}) collective-permute-start(f32[2,128,256]{2,1,0:T(8,128)S(1)} %pad_maximum_fusion.3), channel_id=1, source_target_pairs={{496,0},{504,8},{0,16},{8,24},{16,32},{24,40},{32,48},{40,56},{48,... | collective-permute-start | bytes 786440 | tf_op jit(solution)/shard_map/ppermute | solution.py:18
  165.6 1.4 copy-start.2
  165.6 1.4 copy-start.5
Sparse Core Ops, SparseCore 0:
  167.1 225.6 reduce-scatter.1
where the time goes:
time: 408 us; the launch traced here: 403 us
  waiting for transfers between devices  222 us (54%)
  starting transfers between devices  45.1 us (11%)
  between operations  40.7 us (10%)
  matrix products  39.2 us (10%)
  blocking collectives  37.5 us (9%)
  local copies, waits for them, and re-layouts  15.8 us (4%)
    reduce_scatter x1, waiting for transfers between devices, shards(): owned = lax.psum_scatter(arranged, 'seq', scatter_dimension=0, tiled=True)  216 us
    ppermute x12, starting transfers between devices, passed_along(): return lax.ppermute(block, axis, route)  45.1 us
    psum x1, blocking collectives, shards(): lax.psum(running, 'mp').astype(jnp.bfloat16)  37.5 us
    dot_general x20, matrix products, backward(): jnp.einsum('hqk,kd->qhd', dscore, keys_blk, preferred_element_type=jnp.fl...  11.9 us
    dot_general x20, matrix products, tile_scores(): jnp.einsum('qhd,kd->hqk', queries[q_slot], keys_blk, preferred_element_ty...  9.78 us
  transfers between devices with their start and end apart: 13, of which 3 were waited for; matrix products, arithmetic and copies ran while one was open for 8% of the time, Pallas kernels for 0%

commit v1 on v0

v1 whole, which is shorter than its diff:
```python
import functools
import math

import jax
import jax.numpy as jnp
from jax import lax
from jax.experimental import pallas as pl
from jax.experimental.pallas import tpu as pltpu
from jax.sharding import PartitionSpec as P

BLK = 64
MASKED = -1e30
MESH = pl.DeviceIdType.MESH
F32 = jnp.float32
BF16 = jnp.bfloat16


def contract(a, b, dims):
    return lax.dot_general(a, b, (dims, ((), ())), preferred_element_type=F32)


def kernel(
    n_seq,
    n_mp,
    order_ref,
    owners_ref,
    x_hbm,
    q_ref,
    k_ref,
    v_ref,
    g_ref,
    qg_ref,
    gb_ref,
    left_ref,
    right_ref,
    x_v,
    xt_v,
    inv_v,
    inv_s,
    kv_own,
    kv_in,
    kv_far,
    terms,
    terms_own,
    terms_in,
    pass_near,
    pass_far,
    pass_near_in,
    pass_far_in,
    fin,
    kvg,
    pieces,
    keep,
    core_out,
    core_in,
    y_out,
    y_in,
    z_sum,
    z_out,
    z_in,
    local_sem,
    kv_send,
    kv_recv,
    rs_send,
    rs_recv,
    pass_send,
    pass_recv,
    ag_send,
    ag_recv,
    pair_send,
    pair_recv,
    z_send,
    z_recv,
):
    n_z = n_seq // 4
    rows = q_ref.shape[0]
    half = rows // 2
    hd = q_ref.shape[1]
    cut = half // n_mp
    n_blocks = pieces.shape[0]
    score_scale = 1.0 / math.sqrt(hd)

    s = lax.axis_index("seq")
    m = lax.axis_index("mp")
    core = lax.rem(s, 2)
    y = lax.rem(s // 2, 2)
    z = s // 4

    def place(distance):
        return lax.rem(s + distance + n_seq, n_seq)

    def mate(t):
        return lax.rem(m + t, n_mp)

    x_copy = pltpu.make_async_copy(x_hbm, x_v, local_sem.at[0])
    x_copy.start()

    barrier = pltpu.get_barrier_semaphore()
    partners = [(place(d), m) for d in (1, -1, 2, -2)]
    partners += [(s, mate(t)) for t in range(1, n_mp)]
    partners += [(place(4 * t), m) for t in range(1, n_z)]
    for partner in partners:
        pl.semaphore_signal(barrier, inc=1, device_id=partner, device_id_type=MESH)

    first = order_ref[2 * s]
    following = order_ref[2 * place(1)]
    up = ((following - first + n_seq) & (n_seq - 1)) == 1
    last = first == n_seq - 1
    second_last = first == n_seq - 2

    for slot in range(2):
        kv_own[slot, :, :hd] = k_ref[slot * half : (slot + 1) * half, :]
        kv_own[slot, :, hd:] = v_ref[slot * half : (slot + 1) * half, :]
    kv_far[0] = kv_own[jnp.where(up, 0, 1)]
    kv_far[1] = kv_own[jnp.where(up, 1, 0)]

    pl.semaphore_wait(barrier, len(partners))

    def remote(src, dst, send_sem, recv_sem, to):
        copy = pltpu.make_async_remote_copy(
            src_ref=src,
            dst_ref=dst,
            send_sem=send_sem,
            recv_sem=recv_sem,
            device_id=to,
            device_id_type=MESH,
        )
        copy.start()
        return copy

    started = []
    kv_copies = [
        remote(kv_own, kv_in.at[0:2], kv_send.at[0], kv_recv.at[0], (place(1), m)),
        remote(kv_own, kv_in.at[2:4], kv_send.at[1], kv_recv.at[1], (place(-1), m)),
        remote(kv_far.at[0], kv_in.at[4], kv_send.at[2], kv_recv.at[2], (place(2), m)),
        remote(kv_far.at[1], kv_in.at[5], kv_send.at[3], kv_recv.at[3], (place(-2), m)),
    ]
    started += kv_copies

    spread = jnp.broadcast_to(owners_ref[...], (n_blocks, n_blocks)).T
    slot_of = lax.broadcasted_iota(jnp.int32, (n_blocks, n_blocks), 1)
    block_of = lax.broadcasted_iota(jnp.int32, (n_blocks, n_blocks), 0)
    inv_v[...] = jnp.max(jnp.where(spread == slot_of, block_of, 0), 0, keepdims=True)
    inv_copy = pltpu.make_async_copy(inv_v, inv_s, local_sem.at[1])
    inv_copy.start()

    x_copy.wait()
    xt_v[...] = x_v[...].T
    inv_copy.wait()

    for copy in kv_copies:
        copy.wait_recv()

    row = lax.broadcasted_iota(jnp.int32, (half, half), 0)
    col = lax.broadcasted_iota(jnp.int32, (half, half), 1)
    near_down = jnp.where(up, 0, 2)
    near_up = jnp.where(up, 2, 0)
    before = [
        (kv_in[near_down], kv_in[jnp.where(up, 4, 5)]),
        (
            jnp.where(last, kv_own[0], kv_in[near_up + 1]),
            kv_in[jnp.where(last, near_down, jnp.where(second_last, near_up, jnp.where(up, 5, 4)))],
        ),
    ]
    for slot in range(2):
        window = jnp.concatenate([kv_own[slot], *before[slot]], 0)
        keys, values = window[:, :hd], window[:, hd:]
        queries = q_ref[slot * half : (slot + 1) * half, :]
        grads = g_ref[slot * half : (slot + 1) * half, :]
        position = first if slot == 0 else 2 * n_seq - 1 - first
        visible = jnp.concatenate(
            [
                row - col >= 0,
                jnp.broadcast_to(position >= 1, (half, half)),
                (row - col < 0) & (position >= 2),
            ],
            1,
        )
        scores = jnp.where(visible, contract(queries, keys, ((1,), (1,))) * score_scale, MASKED)
        dprob = contract(grads, values, ((1,), (1,)))
        top = jnp.max(scores, -1, keepdims=True)
        raw = jnp.exp(scores - top)
        prob = raw * (1.0 / jnp.sum(raw, -1, keepdims=True))
        prob_b = prob.astype(BF16)
        delta = jnp.sum(prob_b.astype(F32) * dprob, -1, keepdims=True)
        dscore = (prob * (dprob - delta)).astype(BF16)
        value_grad = contract(prob_b, grads, ((0,), (0,)))
        key_grad = contract(dscore, queries, ((0,), (0,))) * score_scale
        qg_ref[slot * half : (slot + 1) * half, :] = (
            contract(dscore, keys, ((1,), (0,))) * score_scale
        ).astype(BF16)
        for part, index in enumerate((slot, 2 + 2 * slot, 3 + 2 * slot)):
            here = slice(part * half, (part + 1) * half)
            terms_own[index, :, :hd] = key_grad[here]
            terms_own[index, :, hd:] = value_grad[here]
            terms[index, :, :hd] = key_grad[here].astype(BF16)
            terms[index, :, hd:] = value_grad[here].astype(BF16)

    rs_copies = [
        remote(
            terms.at[:, pl.ds(pl.multiple_of(mate(t) * cut, cut), cut), :],
            terms_in.at[t - 1],
            rs_send.at[t - 1],
            rs_recv.at[t - 1],
            (s, mate(t)),
        )
        for t in range(1, n_mp)
    ]
    started += rs_copies
    my_rows = pl.ds(pl.multiple_of(m * cut, cut), cut)
    total = terms_own[:, my_rows, :]
    for t in range(1, n_mp):
        rs_copies[t - 1].wait_recv()
        total = total + terms_in[t - 1].astype(F32)

    own0, own1, down1, down2, up1, up2 = [total[i] for i in range(6)]
    own0 = own0 + jnp.where(last, up1, 0.0)
    down1 = down1 + jnp.where(last, up2, 0.0)
    up1 = jnp.where(last, 0.0, up1)
    crossing = jnp.where(second_last, up2, 0.0)
    up2 = jnp.where(last | second_last, 0.0, up2)
    nothing = jnp.zeros_like(own0)
    pass_near[0, 0] = jnp.where(up, crossing, down1).astype(BF16)
    pass_near[0, 1] = jnp.where(up, up1, nothing).astype(BF16)
    pass_near[1, 0] = jnp.where(up, down1, crossing).astype(BF16)
    pass_near[1, 1] = jnp.where(up, nothing, up1).astype(BF16)
    pass_far[0] = jnp.where(up, up2, down2).astype(BF16)
    pass_far[1] = jnp.where(up, down2, up2).astype(BF16)
    pass_copies = [
        remote(pass_near.at[0], pass_near_in.at[0], pass_send.at[0], pass_recv.at[0], (place(1), m)),
        remote(pass_near.at[1], pass_near_in.at[1], pass_send.at[1], pass_recv.at[1], (place(-1), m)),
        remote(pass_far.at[0], pass_far_in.at[0], pass_send.at[2], pass_recv.at[2], (place(2), m)),
        remote(pass_far.at[1], pass_far_in.at[1], pass_send.at[3], pass_recv.at[3], (place(-2), m)),
    ]
    started += pass_copies
    for copy in pass_copies:
        copy.wait_recv()
    from_before = pass_far_in[0].astype(F32)
    from_after = pass_far_in[1].astype(F32)
    near = pass_near_in[0].astype(F32) + pass_near_in[1].astype(F32)
    own0 = own0 + near[0] + jnp.where(up, from_after, from_before)
    own1 = own1 + near[1] + jnp.where(up, from_before, from_after)
    fin[0] = own0.astype(BF16)
    fin[1] = own1.astype(BF16)
    kvg[:, my_rows, :] = fin[...]
    ag_copies = [
        remote(fin, kvg.at[:, my_rows, :], ag_send.at[t - 1], ag_recv.at[t - 1], (s, mate(t)))
        for t in range(1, n_mp)
    ]
    started += ag_copies
    for copy in ag_copies:
        copy.wait_recv()

    kv_grad = kvg[...].reshape(rows, 2 * hd)
    lane = lax.broadcasted_iota(jnp.int32, (BLK // 2, 2 * BLK), 1)
    weight_scale = 1.0 / math.sqrt(rows * n_seq)
    step = min(4, n_blocks // 4)

    @pl.loop(0, n_blocks // (4 * step))
    def _(i):
        here = pl.ds(pl.multiple_of(i * step * BLK, step * BLK), step * BLK)
        part = contract(xt_v[here, :], kv_grad, ((1,), (0,))) * weight_scale
        for r in range(step):
            for j in range(2):
                tile = part[r * BLK : (r + 1) * BLK, j * 2 * BLK : (j + 1) * 2 * BLK]
                upper, lower = tile[: BLK // 2], tile[BLK // 2 :]
                pieces[(i * step + r) * 4 + 2 * j] = jnp.where(
                    lane < BLK, upper, pltpu.roll(lower, BLK, 1)
                )
                pieces[(i * step + r) * 4 + 2 * j + 1] = jnp.where(
                    lane < BLK, pltpu.roll(upper, BLK, 1), lower
                )

    @pl.loop(0, 2 * n_z)
    def _(j):
        slot = 2 * (2 * lax.rem(j, n_z) + j // n_z)
        core_out[j] = pieces[inv_s[0, slot + 1 - core] & (n_blocks - 1)].astype(BF16)

    core_copy = remote(core_out, core_in, pair_send.at[0], pair_recv.at[0], (s + 1 - 2 * core, m))
    started.append(core_copy)

    @pl.loop(0, 2 * n_z)
    def _(j):
        slot = 2 * (2 * lax.rem(j, n_z) + j // n_z)
        keep[j] = pieces[inv_s[0, slot + core] & (n_blocks - 1)]

    core_copy.wait_recv()
    theirs = pl.ds((1 - y) * n_z, n_z)
    y_out[...] = (keep[theirs] + core_in[theirs].astype(F32)).astype(BF16)
    y_copy = remote(y_out, y_in, pair_send.at[1], pair_recv.at[1], (s + 2 - 4 * y, m))
    started.append(y_copy)
    ours = pl.ds(y * n_z, n_z)
    z_sum[...] = keep[ours] + core_in[ours].astype(F32)
    y_copy.wait_recv()
    z_sum[...] += y_in[...].astype(F32)
    z_out[...] = z_sum[...].astype(BF16)
    z_copies = [
        remote(
            z_out.at[lax.rem(z + t, n_z)],
            z_in.at[t - 1],
            z_send.at[t - 1],
            z_recv.at[t - 1],
            (place(4 * t), m),
        )
        for t in range(1, n_z)
    ]
    started += z_copies
    owned = z_sum[z]
    for t in range(1, n_z):
        z_copies[t - 1].wait_recv()
        owned = owned + z_in[t - 1].astype(F32)

    block = jnp.concatenate([owned[:, :BLK], owned[:, BLK:]], 0)
    gb_ref[0, 0] = block

    def exact(dims):
        return (
            lax.dot_general(
                block,
                block,
                (dims, ((), ())),
                precision=lax.Precision.HIGHEST,
                preferred_element_type=F32,
            )
            / BLK
        )

    left_ref[0, 0] = exact(((1,), (1,)))
    right_ref[0, 0] = exact(((0,), (0,)))
    for copy in started:
        copy.wait_send()


def shards(n_seq, n_mp, layer_input, query_heads, key_head, value_head, attn_grad, block_order, owners):
    rows, columns = layer_input.shape
    half = rows // 2
    hd = key_head.shape[1]
    cut = half // n_mp
    n_z = n_seq // 4
    n_blocks = owners.shape[1]
    shape = (BLK // 2, 2 * BLK)
    vmem = pl.BlockSpec(memory_space=pltpu.VMEM)
    stat = jax.ShapeDtypeStruct((1, 1, BLK, BLK), F32)
    dma = pltpu.SemaphoreType.DMA
    return pl.pallas_call(
        functools.partial(kernel, n_seq, n_mp),
        out_shape=(jax.ShapeDtypeStruct((rows, hd), BF16), stat, stat, stat),
        in_specs=[
            pl.BlockSpec(memory_space=pltpu.SMEM),
            vmem,
            pl.BlockSpec(memory_space=pl.ANY),
            vmem,
            vmem,
            vmem,
            vmem,
        ],
        out_specs=(vmem, vmem, vmem, vmem),
        scratch_shapes=[
            pltpu.VMEM((rows, columns), BF16),
            pltpu.VMEM((columns, rows), BF16),
            pltpu.VMEM((1, n_blocks), jnp.int32),
            pltpu.SMEM((1, n_blocks), jnp.int32),
            pltpu.VMEM((2, half, 2 * hd), BF16),
            pltpu.VMEM((6, half, 2 * hd), BF16),
            pltpu.VMEM((2, half, 2 * hd), BF16),
            pltpu.VMEM((6, half, 2 * hd), BF16),
            pltpu.VMEM((6, half, 2 * hd), F32),
            pltpu.VMEM((n_mp - 1, 6, cut, 2 * hd), BF16),
            pltpu.VMEM((2, 2, cut, 2 * hd), BF16),
            pltpu.VMEM((2, cut, 2 * hd), BF16),
            pltpu.VMEM((2, 2, cut, 2 * hd), BF16),
            pltpu.VMEM((2, cut, 2 * hd), BF16),
            pltpu.VMEM((2, cut, 2 * hd), BF16),
            pltpu.VMEM((2, half, 2 * hd), BF16),
            pltpu.VMEM((n_blocks, *shape), F32),
            pltpu.VMEM((2 * n_z, *shape), F32),
            pltpu.VMEM((2 * n_z, *shape), BF16),
            pltpu.VMEM((2 * n_z, *shape), BF16),
            pltpu.VMEM((n_z, *shape), BF16),
            pltpu.VMEM((n_z, *shape), BF16),
            pltpu.VMEM((n_z, *shape), F32),
            pltpu.VMEM((n_z, *shape), BF16),
            pltpu.VMEM((n_z - 1, *shape), BF16),
            dma((2,)),
            dma((4,)),
            dma((4,)),
            dma((n_mp - 1,)),
            dma((n_mp - 1,)),
            dma((4,)),
            dma((4,)),
            dma((n_mp - 1,)),
            dma((n_mp - 1,)),
            dma((2,)),
            dma((2,)),
            dma((n_z - 1,)),
            dma((n_z - 1,)),
        ],
        compiler_params=pltpu.CompilerParams(
            collective_id=0, has_side_effects=True, vmem_limit_bytes=32 * 1024 * 1024
        ),
    )(block_order, owners, layer_input, query_heads, key_head, value_head, attn_grad)


def solution(mesh):
    return jax.shard_map(
        functools.partial(shards, mesh.shape["seq"], mesh.shape["mp"]),
        mesh=mesh,
        in_specs=(
            P("seq", "mp"),
            P("seq", "mp"),
            P("seq", None),
            P("seq", None),
            P("seq", "mp"),
            P(),
            P("mp", None),
        ),
        out_specs=(
            P("seq", "mp"),
            P("mp", "seq", None, None),
            P("mp", "seq", None, None),
            P("mp", "seq", None, None),
        ),
        check_vma=False,
    )
```

time: 408 us -> 68.6 us (0.17)
  the two profiles are of different devices: /device:TPU:1 before, /device:TPU:8 now
where the time goes in v1:
time: 68.6 us; the launch traced here: 68.3 us
  Pallas kernels  59.4 us (87%)
  local copies, waits for them, and re-layouts  8.17 us (12%)
    pallas_call x1, Pallas kernels, shards(): pl.pallas_call(functools.partial(kernel, n_seq, n_mp), out_shape=(jax.Sha...  59.4 us
    unnamed x18, local copies, waits for them, and re-layouts  8.17 us

profile of v1, /device:TPU:8, one launch (start us, length us, event | category | flops | bytes accessed | tf_op | source)
XLA Modules:
  0.0 68.3 jit_solution(6154137551098816984)
XLA Ops:
  0.6 0.0 copy-start
  0.6 1.0 %copy-done = bf16[256,1024]{1,0:T(8,128)(2,1)S(1)} copy-done((bf16[256,1024]{1,0:T(8,128)(2,1)S(1)}, bf16[256,1024]{1,0:T(8,128)(2,1)}, u32[]{:S(2)}) %copy-start) | copy-done | bytes 524312
  1.7 0.0 copy-start.1
  1.7 0.8 %copy-done.1 = bf16[256,128]{1,0:T(8,128)(2,1)S(1)} copy-done((bf16[256,128]{1,0:T(8,128)(2,1)S(1)}, bf16[256,128]{1,0:T(8,128)(2,1)}, u32[]{:S(2)}) %copy-start.1) | copy-done | bytes 65560
  2.5 0.0 copy-start.2
  2.5 0.8 %copy-done.2 = bf16[256,128]{1,0:T(8,128)(2,1)S(1)} copy-done((bf16[256,128]{1,0:T(8,128)(2,1)S(1)}, bf16[256,128]{1,0:T(8,128)(2,1)}, u32[]{:S(2)}) %copy-start.2) | copy-done | bytes 65560
  3.4 0.0 copy-start.3
  3.4 0.8 %copy-done.3 = bf16[256,128]{1,0:T(8,128)(2,1)S(1)} copy-done((bf16[256,128]{1,0:T(8,128)(2,1)S(1)}, bf16[256,128]{1,0:T(8,128)(2,1)}, u32[]{:S(2)}) %copy-start.3) | copy-done | bytes 65560
  4.2 0.0 copy-start.4
  4.2 0.8 %copy-done.4 = bf16[256,128]{1,0:T(8,128)(2,1)S(1)} copy-done((bf16[256,128]{1,0:T(8,128)(2,1)S(1)}, bf16[256,128]{1,0:T(8,128)(2,1)}, u32[]{:S(2)}) %copy-start.4) | copy-done | bytes 65560
  5.0 0.0 copy-start.5
  5.0 0.7 copy-done.5
  5.7 0.0 copy-start.6
  5.7 0.7 copy-done.6
  6.3 59.4 %shard_map.102 = (bf16[256,128]{1,0:T(8,128)(2,1)S(1)}, f32[1,1,64,64]{3,2,1,0:T(8,128)S(1)}, f32[1,1,64,64]{3,2,1,0:T(8,128)S(1)}, f32[1,1,64,64]{3,2,1,0:T(8,128)S(1)}) custom-call(s32[128]{0:T(128)S(1)} %copy-done.5, s32[1,64]{1,0:T(1,128)S(1)} %copy-done.6, bf16[256,1024]{1,0:T(8,128)(2,1)S(1)} %copy-done, bf16[256,128]{1,0:T(8,128)(2,1)S(1)} %copy-done.1, ...), custom_call_target="tpu_custom_call" | custom-call | tf_op jit(solution)/shard_map/pallas_call | solution.py:345
  65.8 0.6 copy.15
  66.4 0.6 copy.16
  67.0 0.6 copy.17
  67.6 0.6 copy.18
Async XLA Ops:
  0.6 1.0 %copy-start = (bf16[256,1024]{1,0:T(8,128)(2,1)S(1)}, bf16[256,1024]{1,0:T(8,128)(2,1)}, u32[]{:S(2)}) copy-start(bf16[256,1024]{1,0:T(8,128)(2,1)} %x_hbm.1) | copy-start | bytes 1572868
  1.7 0.8 %copy-start.1 = (bf16[256,128]{1,0:T(8,128)(2,1)S(1)}, bf16[256,128]{1,0:T(8,128)(2,1)}, u32[]{:S(2)}) copy-start(bf16[256,128]{1,0:T(8,128)(2,1)} %q_ref.1) | copy-start | bytes 196612
  2.5 0.8 %copy-start.2 = (bf16[256,128]{1,0:T(8,128)(2,1)S(1)}, bf16[256,128]{1,0:T(8,128)(2,1)}, u32[]{:S(2)}) copy-start(bf16[256,128]{1,0:T(8,128)(2,1)} %k_ref.1) | copy-start | bytes 196612
  3.4 0.8 %copy-start.3 = (bf16[256,128]{1,0:T(8,128)(2,1)S(1)}, bf16[256,128]{1,0:T(8,128)(2,1)}, u32[]{:S(2)}) copy-start(bf16[256,128]{1,0:T(8,128)(2,1)} %v_ref.1) | copy-start | bytes 196612
  4.2 0.8 %copy-start.4 = (bf16[256,128]{1,0:T(8,128)(2,1)S(1)}, bf16[256,128]{1,0:T(8,128)(2,1)}, u32[]{:S(2)}) copy-start(bf16[256,128]{1,0:T(8,128)(2,1)} %g_ref.1) | copy-start | bytes 196612
  5.0 0.7 copy-start.5
  5.7 0.7 copy-start.6

commit v2 on v1

v2 whole, which is shorter than its diff:
```python
import functools
import math

import jax
import jax.numpy as jnp
from jax import lax
from jax.experimental import pallas as pl
from jax.experimental.pallas import tpu as pltpu
from jax.sharding import PartitionSpec as P

BLK = 64
STEP = 4
PARTS = 4
MASKED = -1e30
MESH = pl.DeviceIdType.MESH
F32 = jnp.float32
BF16 = jnp.bfloat16


def contract(a, b, dims):
    return lax.dot_general(a, b, (dims, ((), ())), preferred_element_type=F32)


def kernel(
    n_seq,
    n_mp,
    order_hbm,
    owners_hbm,
    x_hbm,
    q_hbm,
    k_hbm,
    v_hbm,
    g_hbm,
    qg_ref,
    sum_ref,
    order_ref,
    owners_ref,
    q_ref,
    g_ref,
    x_v,
    xt_v,
    inv_v,
    inv_s,
    kv_own,
    kv_sel,
    kv_in,
    kv_other,
    terms,
    terms_own,
    terms_in,
    pass_near,
    pass_far,
    pass_near_in,
    pass_far_in,
    fin,
    kvg,
    pieces,
    keep,
    core_out,
    core_in,
    y_out,
    y_in,
    z_out,
    z_in,
    load_sem,
    word_sem,
    kv_send,
    kv_recv,
    rs_send,
    rs_recv,
    pass_send,
    pass_recv,
    ag_send,
    ag_recv,
    core_send,
    core_recv,
    y_send,
    y_recv,
    z_send,
    z_recv,
):
    n_z = n_seq // 4
    rows = q_ref.shape[0]
    half = rows // 2
    hd = q_ref.shape[1]
    cut = half // n_mp
    n_blocks = pieces.shape[0]
    score_scale = 1.0 / math.sqrt(hd)

    s = lax.axis_index("seq")
    m = lax.axis_index("mp")
    core = lax.rem(s, 2)
    y = lax.rem(s // 2, 2)
    z = s // 4

    def place(distance):
        return lax.rem(s + distance + n_seq, n_seq)

    n_x = min(4, n_mp)
    offsets = sorted(
        [(a, b) for a in range(n_mp // n_x) for b in range(n_x) if a + b > 0],
        key=lambda o: -(2 * o[0] + min(o[1], n_x - o[1])),
    )

    def mate(offset):
        a, b = offset
        return lax.rem(m // n_x + a, n_mp // n_x) * n_x + lax.rem(lax.rem(m, n_x) + b, n_x)

    loads = [
        pltpu.make_async_copy(src, dst, load_sem.at[i])
        for i, (src, dst) in enumerate(
            [
                (order_hbm, order_ref),
                (k_hbm.at[0:half], kv_own.at[0, 0]),
                (v_hbm.at[0:half], kv_own.at[0, 1]),
                (k_hbm.at[half:rows], kv_own.at[1, 0]),
                (v_hbm.at[half:rows], kv_own.at[1, 1]),
                (owners_hbm, owners_ref),
                (q_hbm, q_ref),
                (g_hbm, g_ref),
                (x_hbm, x_v),
            ]
        )
    ]
    for load in loads:
        load.start()

    barrier = pltpu.get_barrier_semaphore()
    next_x = sorted({(0, 1), (0, n_x - 1)} - {(0, 0)})
    all_x = [(0, b) for b in range(1, n_x)]
    other_y = [(a, 0) for a in range(1, n_mp // n_x)]
    next_z = [(place(4 * t), m) for t in sorted({1, n_z - 1})]
    partners = [(place(d), m) for d in (1, -1, 2, -2)] + next_z
    partners += [(s, mate(o)) for o in next_x + other_y]
    reaches = [1 << i for i in range((n_z // 2).bit_length() - 1)]
    along_z = [[(place(4 * t), m) for t in (r, n_z - r)] for r in reaches[1:]]
    rounds = [partners, [(s, mate(o)) for o in all_x] + sum(along_z[:1], []), *along_z[1:]]

    def tell(i):
        for partner in rounds[i]:
            pl.semaphore_signal(
                word_sem.at[i], inc=1, device_id=partner, device_id_type=MESH
            )

    def heard(i):
        pl.semaphore_wait(word_sem.at[i], len(rounds[i]))

    for partner in partners:
        pl.semaphore_signal(barrier, inc=1, device_id=partner, device_id_type=MESH)

    for load in loads[:5]:
        load.wait()

    first = order_ref[2 * s]
    following = order_ref[2 * place(1)]
    up = ((following - first + n_seq) & (n_seq - 1)) == 1
    last = first == n_seq - 1
    second_last = first == n_seq - 2

    kv_sel[0] = kv_own[jnp.where(up, 0, 1)]
    kv_sel[1] = kv_own[jnp.where(up, 1, 0)]

    pl.semaphore_wait(barrier, len(partners))

    def remote(src, dst, send_sem, recv_sem, to):
        copy = pltpu.make_async_remote_copy(
            src_ref=src,
            dst_ref=dst,
            send_sem=send_sem,
            recv_sem=recv_sem,
            device_id=to,
            device_id_type=MESH,
        )
        copy.start()
        return copy

    started = []
    kv_copies = [
        remote(kv_sel.at[0], kv_in.at[2], kv_send.at[0], kv_recv.at[0], (place(2), m)),
        remote(kv_sel.at[1], kv_in.at[3], kv_send.at[1], kv_recv.at[1], (place(-2), m)),
        remote(kv_sel.at[0], kv_in.at[0], kv_send.at[2], kv_recv.at[2], (place(1), m)),
        remote(kv_sel.at[1], kv_in.at[1], kv_send.at[3], kv_recv.at[3], (place(-1), m)),
        remote(kv_sel.at[1], kv_other.at[0], kv_send.at[4], kv_recv.at[4], (place(1), m)),
        remote(kv_sel.at[0], kv_other.at[1], kv_send.at[5], kv_recv.at[5], (place(-1), m)),
    ]
    started += kv_copies
    tell(0)

    loads[5].wait()
    spread = jnp.broadcast_to(owners_ref[...], (n_blocks, n_blocks)).T
    slot_of = lax.broadcasted_iota(jnp.int32, (n_blocks, n_blocks), 1)
    block_of = lax.broadcasted_iota(jnp.int32, (n_blocks, n_blocks), 0)
    inv_v[...] = jnp.max(jnp.where(spread == slot_of, block_of, 0), 0, keepdims=True)
    inv_copy = pltpu.make_async_copy(inv_v, inv_s, load_sem.at[9])
    inv_copy.start()

    for load in loads[6:]:
        load.wait()
    xt_v[...] = x_v[...].T
    inv_copy.wait()

    heard(0)
    tell(1)
    for copy in kv_copies[:4]:
        copy.wait_recv()

    row = lax.broadcasted_iota(jnp.int32, (half, half), 0)
    col = lax.broadcasted_iota(jnp.int32, (half, half), 1)
    rs_copies = []
    for slot in range(2):
        if slot == 0:
            window = [kv_own[0], kv_in[jnp.where(up, 0, 1)], kv_in[jnp.where(up, 2, 3)]]
        else:
            for copy in kv_copies[4:]:
                copy.wait_recv()
            window = [
                kv_own[1],
                jnp.where(last, kv_own[0], kv_in[jnp.where(up, 1, 0)]),
                jnp.where(
                    second_last,
                    kv_other[jnp.where(up, 1, 0)],
                    kv_in[jnp.where(last, jnp.where(up, 0, 1), jnp.where(up, 3, 2))],
                ),
            ]
        keys = jnp.concatenate([pair[0] for pair in window], 0)
        values = jnp.concatenate([pair[1] for pair in window], 0)
        queries = q_ref[slot * half : (slot + 1) * half, :]
        grads = g_ref[slot * half : (slot + 1) * half, :]
        position = first if slot == 0 else 2 * n_seq - 1 - first
        visible = jnp.concatenate(
            [
                row - col >= 0,
                jnp.broadcast_to(position >= 1, (half, half)),
                (row - col < 0) & (position >= 2),
            ],
            1,
        )
        scores = jnp.where(visible, contract(queries, keys, ((1,), (1,))) * score_scale, MASKED)
        dprob = contract(grads, values, ((1,), (1,)))
        top = jnp.max(scores, -1, keepdims=True)
        raw = jnp.exp(scores - top)
        prob = raw * (1.0 / jnp.sum(raw, -1, keepdims=True))
        prob_b = prob.astype(BF16)
        delta = jnp.sum(prob_b.astype(F32) * dprob, -1, keepdims=True)
        dscore = (prob * (dprob - delta)).astype(BF16)
        value_grad = contract(prob_b, grads, ((0,), (0,)))
        key_grad = contract(dscore, queries, ((0,), (0,))) * score_scale
        qg_ref[slot * half : (slot + 1) * half, :] = (
            contract(dscore, keys, ((1,), (0,))) * score_scale
        ).astype(BF16)
        for part in range(3):
            here = slice(part * half, (part + 1) * half)
            terms_own[3 * slot + part, :, :hd] = key_grad[here]
            terms_own[3 * slot + part, :, hd:] = value_grad[here]
            terms[3 * slot + part, :, :hd] = key_grad[here].astype(BF16)
            terms[3 * slot + part, :, hd:] = value_grad[here].astype(BF16)

        if slot == 0:
            heard(1)
            for i in range(2, len(rounds)):
                tell(i)
        these = pl.ds(3 * slot, 3)
        rs_copies.append(
            [
                remote(
                    terms.at[these, pl.ds(pl.multiple_of(mate(offsets[i]) * cut, cut), cut), :],
                    terms_in.at[i, these],
                    rs_send.at[slot, i],
                    rs_recv.at[slot, i],
                    (s, mate(offsets[i])),
                )
                for i in range(n_mp - 1)
            ]
        )
        started += rs_copies[-1]
    my_rows = pl.ds(pl.multiple_of(m * cut, cut), cut)
    total = []
    for slot in range(2):
        part = terms_own[3 * slot : 3 * slot + 3, my_rows, :]
        for i in reversed(range(n_mp - 1)):
            rs_copies[slot][i].wait_recv()
            part = part + terms_in[i, 3 * slot : 3 * slot + 3].astype(F32)
        total += [part[0], part[1], part[2]]

    own0, down1, down2, own1, up1, up2 = total
    own0 = own0 + jnp.where(last, up1, 0.0)
    down1 = down1 + jnp.where(last, up2, 0.0)
    up1 = jnp.where(last, 0.0, up1)
    crossing = jnp.where(second_last, up2, 0.0)
    up2 = jnp.where(last | second_last, 0.0, up2)
    nothing = jnp.zeros_like(own0)
    pass_near[0, 0] = jnp.where(up, crossing, down1).astype(BF16)
    pass_near[0, 1] = jnp.where(up, up1, nothing).astype(BF16)
    pass_near[1, 0] = jnp.where(up, down1, crossing).astype(BF16)
    pass_near[1, 1] = jnp.where(up, nothing, up1).astype(BF16)
    pass_far[0] = jnp.where(up, up2, down2).astype(BF16)
    pass_far[1] = jnp.where(up, down2, up2).astype(BF16)
    pass_copies = [
        remote(pass_near.at[0], pass_near_in.at[0], pass_send.at[0], pass_recv.at[0], (place(1), m)),
        remote(pass_near.at[1], pass_near_in.at[1], pass_send.at[1], pass_recv.at[1], (place(-1), m)),
        remote(pass_far.at[0], pass_far_in.at[0], pass_send.at[2], pass_recv.at[2], (place(2), m)),
        remote(pass_far.at[1], pass_far_in.at[1], pass_send.at[3], pass_recv.at[3], (place(-2), m)),
    ]
    started += pass_copies
    for copy in pass_copies:
        copy.wait_recv()
    from_before = pass_far_in[0].astype(F32)
    from_after = pass_far_in[1].astype(F32)
    near = pass_near_in[0].astype(F32) + pass_near_in[1].astype(F32)
    own0 = own0 + near[0] + jnp.where(up, from_after, from_before)
    own1 = own1 + near[1] + jnp.where(up, from_before, from_after)
    fin[0] = own0.astype(BF16)
    fin[1] = own1.astype(BF16)
    kvg[:, my_rows, :] = fin[...]
    ag_copies = [
        remote(fin, kvg.at[:, my_rows, :], ag_send.at[i], ag_recv.at[i], (s, mate(offsets[i])))
        for i in range(n_mp - 1)
    ]
    started += ag_copies
    for copy in ag_copies:
        copy.wait_recv()

    kv_grad = kvg[...].reshape(rows, 2 * hd)
    lane = lax.broadcasted_iota(jnp.int32, (BLK // 2, 2 * BLK), 1)
    step = min(STEP, n_blocks // 4)
    for i in range(n_blocks // (4 * step)):
        part = contract(xt_v[i * step * BLK : (i + 1) * step * BLK, :], kv_grad, ((1,), (0,)))
        for r in range(step):
            for j in range(2):
                tile = part[r * BLK : (r + 1) * BLK, j * 2 * BLK : (j + 1) * 2 * BLK]
                upper, lower = tile[: BLK // 2], tile[BLK // 2 :]
                pieces[(i * step + r) * 4 + 2 * j] = jnp.where(
                    lane < BLK, upper, pltpu.roll(lower, BLK, 1)
                )
                pieces[(i * step + r) * 4 + 2 * j + 1] = jnp.where(
                    lane < BLK, pltpu.roll(upper, BLK, 1), lower
                )

    def owner_piece(p, whose_y, whose_core):
        t = n_z // 2 + (p + 1) // 2 * (1 - 2 * lax.rem(p, 2))
        slot = 2 * (2 * lax.rem(z + t, n_z) + whose_y) + whose_core
        return pieces[inv_s[0, slot] & (n_blocks - 1)]

    n_parts = min(PARTS, n_z // 2)
    part = n_z // n_parts
    core_copies = []
    for k, whose_y in enumerate((1 - y, y)):
        for c in range(n_parts):

            @pl.loop(c * part, (c + 1) * part, unroll=True)
            def _(p, k=k, whose_y=whose_y):
                core_out[k, p] = owner_piece(p, whose_y, 1 - core).astype(BF16)

            here = pl.ds(c * part, part)
            core_copies.append(
                remote(
                    core_out.at[k, here],
                    core_in.at[k, here],
                    core_send.at[k, c],
                    core_recv.at[k, c],
                    (s + 1 - 2 * core, m),
                )
            )
    for k, whose_y in enumerate((1 - y, y)):

        @pl.loop(0, n_z, unroll=True)
        def _(p, k=k, whose_y=whose_y):
            keep[k, p] = owner_piece(p, whose_y, core)

    y_copies = []
    for c in range(n_parts):
        here = pl.ds(c * part, part)
        core_copies[c].wait_recv()
        y_out[here] = (keep[0, here] + core_in[0, here].astype(F32)).astype(BF16)
        y_copies.append(
            remote(y_out.at[here], y_in.at[here], y_send.at[c], y_recv.at[c], (s + 2 - 4 * y, m))
        )
    for i in range(2, len(rounds)):
        heard(i)
    for copy in started + core_copies:
        copy.wait_send()
    for copy in core_copies[n_parts:]:
        copy.wait_recv()
    z_copies = []
    for c in range(n_parts):
        here = pl.ds(c * part, part)
        ours = keep[1, here] + core_in[1, here].astype(F32)
        y_copies[c].wait_recv()
        ours = ours + y_in[here].astype(F32)
        z_out[here] = ours.astype(BF16)
        for p in range(c * part, min((c + 1) * part, n_z - 1)):
            t = n_z // 2 + (p + 1) // 2 * (1 - 2 * (p % 2))
            z_copies.append(
                remote(z_out.at[p], z_in.at[p], z_send.at[p], z_recv.at[p], (place(4 * t), m))
            )
    for copy in y_copies:
        copy.wait_send()
    owned = ours[part - 1]
    for p in reversed(range(n_z - 1)):
        z_copies[p].wait_recv()
        owned = owned + z_in[p].astype(F32)
    sum_ref[...] = owned
    for copy in z_copies:
        copy.wait_send()


def finish(weight_scale, qg_ref, sum_ref, qg_out, block_out, left_out, right_out):
    qg_out[...] = qg_ref[...]
    owned = sum_ref[...] * weight_scale
    block = jnp.concatenate([owned[:, :BLK], owned[:, BLK:]], 0)
    block_out[0, 0] = block

    def exact(dims):
        return (
            lax.dot_general(
                block,
                block,
                (dims, ((), ())),
                precision=lax.Precision.HIGHEST,
                preferred_element_type=F32,
            )
            / BLK
        )

    left_out[0, 0] = exact(((1,), (1,)))
    right_out[0, 0] = exact(((0,), (0,)))


def shards(n_seq, n_mp, layer_input, query_heads, key_head, value_head, attn_grad, block_order, owners):
    rows, columns = layer_input.shape
    half = rows // 2
    hd = key_head.shape[1]
    cut = half // n_mp
    n_z = n_seq // 4
    n_blocks = owners.shape[1]
    shape = (BLK // 2, 2 * BLK)
    vmem = pl.BlockSpec(memory_space=pltpu.VMEM)
    stat = jax.ShapeDtypeStruct((1, 1, BLK, BLK), F32)
    dma = pltpu.SemaphoreType.DMA
    query_part = jax.ShapeDtypeStruct((rows, hd), BF16)
    query_grad, owned = pl.pallas_call(
        functools.partial(kernel, n_seq, n_mp),
        out_shape=(query_part, jax.ShapeDtypeStruct(shape, F32)),
        in_specs=[pl.BlockSpec(memory_space=pl.ANY)] * 7,
        out_specs=(vmem, vmem),
        scratch_shapes=[
            pltpu.SMEM((2 * n_seq,), jnp.int32),
            pltpu.VMEM((1, n_blocks), jnp.int32),
            pltpu.VMEM((rows, hd), BF16),
            pltpu.VMEM((rows, hd), BF16),
            pltpu.VMEM((rows, columns), BF16),
            pltpu.VMEM((columns, rows), BF16),
            pltpu.VMEM((1, n_blocks), jnp.int32),
            pltpu.SMEM((1, n_blocks), jnp.int32),
            pltpu.VMEM((2, 2, half, hd), BF16),
            pltpu.VMEM((2, 2, half, hd), BF16),
            pltpu.VMEM((4, 2, half, hd), BF16),
            pltpu.VMEM((2, 2, half, hd), BF16),
            pltpu.VMEM((6, half, 2 * hd), BF16),
            pltpu.VMEM((6, half, 2 * hd), F32),
            pltpu.VMEM((n_mp - 1, 6, cut, 2 * hd), BF16),
            pltpu.VMEM((2, 2, cut, 2 * hd), BF16),
            pltpu.VMEM((2, cut, 2 * hd), BF16),
            pltpu.VMEM((2, 2, cut, 2 * hd), BF16),
            pltpu.VMEM((2, cut, 2 * hd), BF16),
            pltpu.VMEM((2, cut, 2 * hd), BF16),
            pltpu.VMEM((2, half, 2 * hd), BF16),
            pltpu.VMEM((n_blocks, *shape), F32),
            pltpu.VMEM((2, n_z, *shape), F32),
            pltpu.VMEM((2, n_z, *shape), BF16),
            pltpu.VMEM((2, n_z, *shape), BF16),
            pltpu.VMEM((n_z, *shape), BF16),
            pltpu.VMEM((n_z, *shape), BF16),
            pltpu.VMEM((n_z, *shape), BF16),
            pltpu.VMEM((n_z - 1, *shape), BF16),
            dma((10,)),
            pltpu.SemaphoreType.REGULAR((4,)),
            dma((6,)),
            dma((6,)),
            dma((2, n_mp - 1)),
            dma((2, n_mp - 1)),
            dma((4,)),
            dma((4,)),
            dma((n_mp - 1,)),
            dma((n_mp - 1,)),
            dma((2, PARTS)),
            dma((2, PARTS)),
            dma((PARTS,)),
            dma((PARTS,)),
            dma((n_z - 1,)),
            dma((n_z - 1,)),
        ],
        compiler_params=pltpu.CompilerParams(
            collective_id=0, has_side_effects=True, vmem_limit_bytes=60 * 1024 * 1024
        ),
    )(block_order, owners, layer_input, query_heads, key_head, value_head, attn_grad)
    return pl.pallas_call(
        functools.partial(finish, 1.0 / math.sqrt(rows * n_seq)),
        out_shape=(query_part, stat, stat, stat),
        in_specs=[vmem, vmem],
        out_specs=(vmem, vmem, vmem, vmem),
        compiler_params=pltpu.CompilerParams(vmem_limit_bytes=60 * 1024 * 1024),
    )(query_grad, owned)


def solution(mesh):
    return jax.shard_map(
        functools.partial(shards, mesh.shape["seq"], mesh.shape["mp"]),
        mesh=mesh,
        in_specs=(
            P("seq", "mp"),
            P("seq", "mp"),
            P("seq", None),
            P("seq", None),
            P("seq", "mp"),
            P(),
            P("mp", None),
        ),
        out_specs=(
            P("seq", "mp"),
            P("mp", "seq", None, None),
            P("mp", "seq", None, None),
            P("mp", "seq", None, None),
        ),
        check_vma=False,
    )
```

time: 68.6 us -> 54.5 us (0.79)
  the two profiles are of different devices: /device:TPU:8 before, /device:TPU:1 now
where the time goes in v2:
time: 54.5 us; the launch traced here: 54.3 us
  Pallas kernels  53.7 us (99%)
  between operations  0.64 us (1%)
    pallas_call x1, Pallas kernels, shards(): pl.pallas_call(functools.partial(kernel, n_seq, n_mp), out_shape=(query_p...  51.9 us
    pallas_call x1, Pallas kernels, shards(): pl.pallas_call(functools.partial(finish, 1.0 / math.sqrt(rows * n_seq)),...  1.77 us

profile of v2, /device:TPU:1, one launch (start us, length us, event | category | flops | bytes accessed | tf_op | source)
XLA Modules:
  0.0 54.3 jit_solution(17403147412509601600)
XLA Ops:
  0.6 51.9 %shard_map.102 = (bf16[256,128]{1,0:T(8,128)(2,1)}, f32[32,128]{1,0:T(8,128)}) custom-call(s32[128]{0:T(128)} %order_hbm.1, s32[1,64]{1,0:T(1,128)} %owners_hbm.1, bf16[256,1024]{1,0:T(8,128)(2,1)} %x_hbm.1, bf16[256,128]{1,0:T(8,128)(2,1)} %q_hbm.1, bf16[256,128]{1,0:T(8,128)(2,1)} %k_hbm.1, bf16[256,128]{1,0:T(8,128)(2,1)} %v_hbm.1, bf16[256,128]{1,0:T(8,128)(2,1)} %g_hbm.1), custom_call_target="tpu_custom_call" | custom-call | tf_op jit(solution)/shard_map/pallas_call | solution.py:441
  52.6 1.8 %shard_map.103 = (bf16[256,128]{1,0:T(8,128)(2,1)}, f32[1,1,64,64]{3,2,1,0:T(8,128)}, f32[1,1,64,64]{3,2,1,0:T(8,128)}, f32[1,1,64,64]{3,2,1,0:T(8,128)}) custom-call(bf16[256,128]{1,0:T(8,128)(2,1)} %get-tuple-element.6.qg_ref, f32[32,128]{1,0:T(8,128)} %get-tuple-element.7.sum_ref), custom_call_target="tpu_custom_call" | custom-call | tf_op jit(solution)/shard_map/pallas_call | solution.py:497

commit v3 on v2

v3 whole, which is shorter than its diff:
```python
import functools
import math

import jax
import jax.numpy as jnp
from jax import lax
from jax.experimental import pallas as pl
from jax.experimental.pallas import tpu as pltpu
from jax.sharding import PartitionSpec as P

BLK = 64
STEP = 4
PARTS = 4
MASKED = -1e30
MESH = pl.DeviceIdType.MESH
F32 = jnp.float32
BF16 = jnp.bfloat16


def contract(a, b, dims):
    return lax.dot_general(a, b, (dims, ((), ())), preferred_element_type=F32)


def kernel(
    n_seq,
    n_mp,
    order_hbm,
    owners_hbm,
    x_hbm,
    q_hbm,
    k_hbm,
    v_hbm,
    g_hbm,
    qg_hbm,
    sum_ref,
    qg_ref,
    order_ref,
    owners_ref,
    q_ref,
    g_ref,
    x_v,
    xt_v,
    inv_v,
    inv_s,
    k_own,
    k_sel,
    k_in,
    k_other,
    v_own,
    v_sel,
    v_in,
    v_other,
    terms_k,
    terms_v,
    terms_k_in,
    terms_v_in,
    pass_near,
    pass_far,
    pass_near_in,
    pass_far_in,
    own_out,
    own_in,
    kept,
    fin,
    kvg,
    pieces,
    keep,
    far_out,
    far_in,
    core_out,
    core_in,
    y_out,
    y_in,
    z_out,
    z_in,
    load_sem,
    word_sem,
    kv_send,
    kv_recv,
    rs_send,
    rs_recv,
    pass_send,
    pass_recv,
    ag_send,
    ag_recv,
    far_send,
    far_recv,
    core_send,
    core_recv,
    y_send,
    y_recv,
    z_send,
    z_recv,
):
    n_z = n_seq // 4
    rows = q_ref.shape[0]
    half = rows // 2
    hd = q_ref.shape[1]
    n_x = min(4, n_mp)
    n_y = n_mp // n_x
    cut = half // n_x
    n_blocks = pieces.shape[0]
    score_scale = 1.0 / math.sqrt(hd)

    s = lax.axis_index("seq")
    m = lax.axis_index("mp")
    core = lax.rem(s, 2)
    y = lax.rem(s // 2, 2)
    z = s // 4

    def place(distance):
        return lax.rem(s + distance + n_seq, n_seq)

    def mate(a, b):
        return lax.rem(m // n_x + a, n_y) * n_x + lax.rem(lax.rem(m, n_x) + b, n_x)

    along_x = sorted(range(1, n_x), key=lambda b: -min(b, n_x - b))

    barrier = pltpu.get_barrier_semaphore()
    next_z = [(place(4 * t), m) for t in sorted({1, n_z - 1})]
    crossing = {2: y, -2: 1 - y, 1: core * y, -1: (1 - core) * (1 - y)}
    beside = {d: (place(d), lax.rem(m + cross * n_x, n_mp)) for d, cross in crossing.items()}
    partners = list(beside.values()) + next_z
    partners += [(s, mate(0, b)) for b in along_x] + [(s, mate(a, 0)) for a in range(1, n_y)]
    reaches = [1 << i for i in range((n_z // 2).bit_length() - 1)]
    along_z = [[(place(4 * t), m) for t in (r, n_z - r)] for r in reaches[1:]]
    rounds = [partners, *along_z]

    def tell(i):
        for partner in rounds[i]:
            pl.semaphore_signal(
                word_sem.at[i], inc=1, device_id=partner, device_id_type=MESH
            )

    def heard(i):
        pl.semaphore_wait(word_sem.at[i], len(rounds[i]))

    for partner in partners:
        pl.semaphore_signal(barrier, inc=1, device_id=partner, device_id_type=MESH)

    loads = [
        pltpu.make_async_copy(src, dst, load_sem.at[i])
        for i, (src, dst) in enumerate(
            [
                (order_hbm, order_ref),
                (k_hbm.at[0:half], k_own.at[0]),
                (v_hbm.at[0:half], v_own.at[0]),
                (k_hbm.at[half:rows], k_own.at[1]),
                (v_hbm.at[half:rows], v_own.at[1]),
                (owners_hbm, owners_ref),
                (q_hbm, q_ref),
                (g_hbm, g_ref),
                (x_hbm, x_v),
            ]
        )
    ]
    for load in loads:
        load.start()

    for load in loads[:5]:
        load.wait()

    first = order_ref[2 * s]
    following = order_ref[2 * place(1)]
    up = ((following - first + n_seq) & (n_seq - 1)) == 1
    last = first == n_seq - 1
    second_last = first == n_seq - 2

    for own, sel in ((k_own, k_sel), (v_own, v_sel)):
        sel[0] = own[jnp.where(up, 0, 1)]
        sel[1] = own[jnp.where(up, 1, 0)]

    pl.semaphore_wait(barrier, len(partners))

    def remote(src, dst, send_sem, recv_sem, to):
        copy = pltpu.make_async_remote_copy(
            src_ref=src,
            dst_ref=dst,
            send_sem=send_sem,
            recv_sem=recv_sem,
            device_id=to,
            device_id_type=MESH,
        )
        copy.start()
        return copy

    started = []
    def spread_window(j, sel, near_far, other):
        pieces_of = [
            (sel.at[0], near_far.at[2], beside[2]),
            (sel.at[1], near_far.at[3], beside[-2]),
            (sel.at[0], near_far.at[0], beside[1]),
            (sel.at[1], near_far.at[1], beside[-1]),
            (sel.at[1], other.at[0], beside[1]),
            (sel.at[0], other.at[1], beside[-1]),
        ]
        return [
            remote(src, dst, kv_send.at[j, i], kv_recv.at[j, i], to)
            for i, (src, dst, to) in enumerate(pieces_of)
        ]

    k_copies = spread_window(0, k_sel, k_in, k_other)
    v_copies = spread_window(1, v_sel, v_in, v_other)
    started += k_copies + v_copies
    tell(0)

    loads[5].wait()
    spread = jnp.broadcast_to(owners_ref[...], (n_blocks, n_blocks)).T
    slot_of = lax.broadcasted_iota(jnp.int32, (n_blocks, n_blocks), 1)
    block_of = lax.broadcasted_iota(jnp.int32, (n_blocks, n_blocks), 0)
    inv_v[...] = jnp.max(jnp.where(spread == slot_of, block_of, 0), 0, keepdims=True)
    inv_copy = pltpu.make_async_copy(inv_v, inv_s, load_sem.at[9])
    inv_copy.start()

    for load in loads[6:]:
        load.wait()
    xt_v[...] = x_v[...].T
    inv_copy.wait()

    row = lax.broadcasted_iota(jnp.int32, (half, half), 0)
    col = lax.broadcasted_iota(jnp.int32, (half, half), 1)
    queries = [q_ref[slot * half : (slot + 1) * half, :] for slot in range(2)]
    grads = [g_ref[slot * half : (slot + 1) * half, :] for slot in range(2)]
    by_row = ((1,), (1,))
    scores_own = [contract(queries[slot], k_own[slot], by_row) for slot in range(2)]
    dprob_own = [contract(grads[slot], v_own[slot], by_row) for slot in range(2)]

    def before(slot, own, near_far, other):
        if slot == 0:
            blocks = [near_far[jnp.where(up, 0, 1)], near_far[jnp.where(up, 2, 3)]]
        else:
            blocks = [
                jnp.where(last, own[0], near_far[jnp.where(up, 1, 0)]),
                jnp.where(
                    second_last,
                    other[jnp.where(up, 1, 0)],
                    near_far[jnp.where(last, jnp.where(up, 0, 1), jnp.where(up, 3, 2))],
                ),
            ]
        return jnp.concatenate(blocks, 0)

    def send_terms(j, terms, terms_in):
        copies = [
            remote(
                terms.at[:, pl.ds(pl.multiple_of(lax.rem(mate(0, b), n_x) * cut, cut), cut), :],
                terms_in.at[i],
                rs_send.at[j, i],
                rs_recv.at[j, i],
                (s, mate(0, b)),
            )
            for i, b in enumerate(along_x)
        ]
        started.extend(copies)
        return copies

    heard(0)
    for i in range(1, min(2, len(rounds))):
        tell(i)
    for copy in k_copies:
        copy.wait_recv()
    windows = [before(slot, k_own, k_in, k_other) for slot in range(2)]
    probs = []
    probs_b = []
    for slot in range(2):
        position = first if slot == 0 else 2 * n_seq - 1 - first
        visible = jnp.concatenate(
            [
                row - col >= 0,
                jnp.broadcast_to(position >= 1, (half, half)),
                (row - col < 0) & (position >= 2),
            ],
            1,
        )
        scores = jnp.concatenate(
            [scores_own[slot], contract(queries[slot], windows[slot], by_row)], 1
        )
        scores = jnp.where(visible, scores * score_scale, MASKED)
        top = jnp.max(scores, -1, keepdims=True)
        raw = jnp.exp(scores - top)
        probs.append(raw * (1.0 / jnp.sum(raw, -1, keepdims=True)))
        probs_b.append(probs[slot].astype(BF16))
        value_grad = contract(probs_b[slot], grads[slot], ((0,), (0,))).astype(BF16)
        terms_v[3 * slot : 3 * slot + 3] = value_grad.reshape(3, half, hd)
    rs_v_copies = send_terms(0, terms_v, terms_v_in)

    for copy in v_copies:
        copy.wait_recv()
    dscores = []
    for slot in range(2):
        values = before(slot, v_own, v_in, v_other)
        dprob = jnp.concatenate([dprob_own[slot], contract(grads[slot], values, by_row)], 1)
        delta = jnp.sum(probs_b[slot].astype(F32) * dprob, -1, keepdims=True)
        dscores.append((probs[slot] * (dprob - delta)).astype(BF16))
        key_grad = contract(dscores[slot], queries[slot], ((0,), (0,))).astype(BF16)
        terms_k[3 * slot : 3 * slot + 3] = key_grad.reshape(3, half, hd)
    rs_k_copies = send_terms(1, terms_k, terms_k_in)

    for i in range(1, min(2, len(rounds))):
        heard(i)
    for i in range(2, len(rounds)):
        tell(i)
    for slot in range(2):
        query_grad = contract(dscores[slot][:, :half], k_own[slot], ((1,), (0,)))
        query_grad += contract(dscores[slot][:, half:], windows[slot], ((1,), (0,)))
        qg_ref[slot * half : (slot + 1) * half, :] = (query_grad * score_scale).astype(BF16)
    qg_copy = pltpu.make_async_copy(qg_ref, qg_hbm, load_sem.at[10])
    qg_copy.start()

    my_rows = pl.ds(pl.multiple_of(lax.rem(m, n_x) * cut, cut), cut)

    def head_sum(copies, terms, terms_in):
        total = terms[:, my_rows, :].astype(F32)
        for i in reversed(range(n_x - 1)):
            copies[i].wait_recv()
            total = total + terms_in[i].astype(F32)
        return total

    def give_back(j, total):
        own0, down1, down2, own1, up1, up2 = [total[i] for i in range(6)]
        own0 = own0 + jnp.where(last, up1, 0.0)
        down1 = down1 + jnp.where(last, up2, 0.0)
        up1 = jnp.where(last, 0.0, up1)
        across = jnp.where(second_last, up2, 0.0)
        up2 = jnp.where(last | second_last, 0.0, up2)
        nothing = jnp.zeros_like(own0)
        pass_near[j, 0, 0] = jnp.where(up, across, down1).astype(BF16)
        pass_near[j, 0, 1] = jnp.where(up, up1, nothing).astype(BF16)
        pass_near[j, 1, 0] = jnp.where(up, down1, across).astype(BF16)
        pass_near[j, 1, 1] = jnp.where(up, nothing, up1).astype(BF16)
        pass_far[j, 0] = jnp.where(up, up2, down2).astype(BF16)
        pass_far[j, 1] = jnp.where(up, down2, up2).astype(BF16)
        kept[j, 0] = own0
        kept[j, 1] = own1
        own_out[j] = kept[j].astype(BF16)
        returns = [
            (pass_far.at[j, 0], pass_far_in.at[j, 0], place(2), 0),
            (pass_far.at[j, 1], pass_far_in.at[j, 1], place(-2), 1),
            (pass_near.at[j, 0], pass_near_in.at[j, 0], place(1), 2),
            (pass_near.at[j, 1], pass_near_in.at[j, 1], place(-1), 3),
            (own_out.at[j], own_in.at[j], s, 4),
        ]
        copies = [
            remote(src, dst.at[a], pass_send.at[j, i, a], pass_recv.at[j, i, a], (to, mate(a, 0)))
            for a in reversed(range(n_y))
            for src, dst, to, i in returns
            if a > 0 or i < 4
        ]
        started.extend(copies)
        return copies

    def gather(j, copies):
        for copy in copies:
            copy.wait_recv()
        total = kept[j]
        far_before = far_after = 0.0
        for a in range(n_y):
            total = total + pass_near_in[j, 0, a].astype(F32) + pass_near_in[j, 1, a].astype(F32)
            far_before = far_before + pass_far_in[j, 0, a].astype(F32)
            far_after = far_after + pass_far_in[j, 1, a].astype(F32)
            if a > 0:
                total = total + own_in[j, a].astype(F32)
        fin[j, 0] = (total[0] + jnp.where(up, far_after, far_before)).astype(BF16)
        fin[j, 1] = (total[1] + jnp.where(up, far_before, far_after)).astype(BF16)
        kvg[j, :, my_rows, :] = fin[j]
        copies = [
            remote(
                fin.at[j],
                kvg.at[j, :, my_rows, :],
                ag_send.at[j, i],
                ag_recv.at[j, i],
                (s, mate(0, b)),
            )
            for i, b in enumerate(along_x)
        ]
        started.extend(copies)
        return copies

    total_v = head_sum(rs_v_copies, terms_v, terms_v_in)
    pass_v_copies = give_back(1, total_v)
    total_k = head_sum(rs_k_copies, terms_k, terms_k_in) * score_scale
    pass_k_copies = give_back(0, total_k)
    ag_v_copies = gather(1, pass_v_copies)
    ag_k_copies = gather(0, pass_k_copies)

    lane = lax.broadcasted_iota(jnp.int32, (BLK // 2, 2 * BLK), 1)
    step = min(STEP, n_blocks // 4)
    for j, copies in ((1, ag_v_copies), (0, ag_k_copies)):
        for copy in copies:
            copy.wait_recv()
        kv_grad = kvg[j].reshape(rows, hd)
        for i in range(n_blocks // (4 * step)):
            part = contract(xt_v[i * step * BLK : (i + 1) * step * BLK, :], kv_grad, ((1,), (0,)))
            for r in range(step):
                tile = part[r * BLK : (r + 1) * BLK]
                upper, lower = tile[: BLK // 2], tile[BLK // 2 :]
                block = (i * step + r) * 4 + 2 * j
                pieces[block] = jnp.where(lane < BLK, upper, pltpu.roll(lower, BLK, 1))
                pieces[block + 1] = jnp.where(lane < BLK, pltpu.roll(upper, BLK, 1), lower)

    def owner_piece(p, whose_y, whose_core):
        t = n_z // 2 + (p + 1) // 2 * (1 - 2 * (p % 2))
        slot = 2 * (2 * lax.rem(z + t, n_z) + whose_y) + whose_core
        return pieces[inv_s[0, slot] & (n_blocks - 1)]

    n_parts = min(PARTS, n_z // 2)
    part = n_z // n_parts
    far_copies = []
    for g, (dy, dc) in enumerate([(1, 1), (1, 0), (0, 1)]):
        to_y, to_core = lax.rem(y + dy, 2), lax.rem(core + dc, 2)
        for p in range(part):
            far_out[g, p] = owner_piece(p, to_y, to_core).astype(BF16)
        far_copies.append(
            remote(
                far_out.at[g],
                far_in.at[g],
                far_send.at[g],
                far_recv.at[g],
                (4 * z + 2 * to_y + to_core, m),
            )
        )
    core_copies = {}
    for k, whose_y in enumerate((1 - y, y)):
        for c in range(1, n_parts):
            for p in range(c * part, (c + 1) * part):
                core_out[k, p] = owner_piece(p, whose_y, 1 - core).astype(BF16)
            here = pl.ds(c * part, part)
            core_copies[k, c] = remote(
                core_out.at[k, here],
                core_in.at[k, here],
                core_send.at[k, c],
                core_recv.at[k, c],
                (s + 1 - 2 * core, m),
            )
    for p in range(part, n_z):
        keep[0, p] = owner_piece(p, 1 - y, core)
    for p in range(n_z):
        keep[1, p] = owner_piece(p, y, core)

    y_copies = {}
    for c in range(1, n_parts):
        here = pl.ds(c * part, part)
        core_copies[0, c].wait_recv()
        y_out[here] = (keep[0, here] + core_in[0, here].astype(F32)).astype(BF16)
        y_copies[c] = remote(
            y_out.at[here], y_in.at[here], y_send.at[c], y_recv.at[c], (s + 2 - 4 * y, m)
        )
    for i in range(2, len(rounds)):
        heard(i)
    z_copies = []
    for c in range(n_parts):
        here = pl.ds(c * part, part)
        ours = keep[1, here]
        if c == 0:
            for g in (2, 1, 0):
                far_copies[g].wait_recv()
                ours = ours + far_in[g].astype(F32)
        else:
            core_copies[1, c].wait_recv()
            ours = ours + core_in[1, here].astype(F32)
            y_copies[c].wait_recv()
            ours = ours + y_in[here].astype(F32)
        z_out[here] = ours.astype(BF16)
        for p in range(c * part, min((c + 1) * part, n_z - 1)):
            t = n_z // 2 + (p + 1) // 2 * (1 - 2 * (p % 2))
            z_copies.append(
                remote(z_out.at[p], z_in.at[p], z_send.at[p], z_recv.at[p], (place(4 * t), m))
            )
    for copy in [*started, *far_copies, *core_copies.values(), *y_copies.values()]:
        copy.wait_send()
    qg_copy.wait()
    owned = ours[part - 1]
    for p in reversed(range(n_z - 1)):
        z_copies[p].wait_recv()
        owned = owned + z_in[p].astype(F32)
    sum_ref[...] = owned
    for copy in z_copies:
        copy.wait_send()


def finish(weight_scale, qg_ref, sum_ref, qg_out, block_out, left_out, right_out):
    qg_out[...] = qg_ref[...]
    owned = sum_ref[...] * weight_scale
    block = jnp.concatenate([owned[:, :BLK], owned[:, BLK:]], 0)
    block_out[0, 0] = block

    def exact(dims):
        return (
            lax.dot_general(
                block,
                block,
                (dims, ((), ())),
                precision=lax.Precision.HIGHEST,
                preferred_element_type=F32,
            )
            / BLK
        )

    left_out[0, 0] = exact(((1,), (1,)))
    right_out[0, 0] = exact(((0,), (0,)))


def shards(n_seq, n_mp, layer_input, query_heads, key_head, value_head, attn_grad, block_order, owners):
    rows, columns = layer_input.shape
    half = rows // 2
    hd = key_head.shape[1]
    n_x = min(4, n_mp)
    n_y = n_mp // n_x
    cut = half // n_x
    n_z = n_seq // 4
    n_blocks = owners.shape[1]
    shape = (BLK // 2, 2 * BLK)
    vmem = pl.BlockSpec(memory_space=pltpu.VMEM)
    stat = jax.ShapeDtypeStruct((1, 1, BLK, BLK), F32)
    dma = pltpu.SemaphoreType.DMA
    query_part = jax.ShapeDtypeStruct((rows, hd), BF16)
    query_grad, owned = pl.pallas_call(
        functools.partial(kernel, n_seq, n_mp),
        out_shape=(query_part, jax.ShapeDtypeStruct(shape, F32)),
        in_specs=[pl.BlockSpec(memory_space=pl.ANY)] * 7,
        out_specs=(pl.BlockSpec(memory_space=pl.ANY), vmem),
        scratch_shapes=[
            pltpu.VMEM((rows, hd), BF16),
            pltpu.SMEM((2 * n_seq,), jnp.int32),
            pltpu.VMEM((1, n_blocks), jnp.int32),
            pltpu.VMEM((rows, hd), BF16),
            pltpu.VMEM((rows, hd), BF16),
            pltpu.VMEM((rows, columns), BF16),
            pltpu.VMEM((columns, rows), BF16),
            pltpu.VMEM((1, n_blocks), jnp.int32),
            pltpu.SMEM((1, n_blocks), jnp.int32),
            pltpu.VMEM((2, half, hd), BF16),
            pltpu.VMEM((2, half, hd), BF16),
            pltpu.VMEM((4, half, hd), BF16),
            pltpu.VMEM((2, half, hd), BF16),
            pltpu.VMEM((2, half, hd), BF16),
            pltpu.VMEM((2, half, hd), BF16),
            pltpu.VMEM((4, half, hd), BF16),
            pltpu.VMEM((2, half, hd), BF16),
            pltpu.VMEM((6, half, hd), BF16),
            pltpu.VMEM((6, half, hd), BF16),
            pltpu.VMEM((n_x - 1, 6, cut, hd), BF16),
            pltpu.VMEM((n_x - 1, 6, cut, hd), BF16),
            pltpu.VMEM((2, 2, 2, cut, hd), BF16),
            pltpu.VMEM((2, 2, cut, hd), BF16),
            pltpu.VMEM((2, 2, n_y, 2, cut, hd), BF16),
            pltpu.VMEM((2, 2, n_y, cut, hd), BF16),
            pltpu.VMEM((2, 2, cut, hd), BF16),
            pltpu.VMEM((2, n_y, 2, cut, hd), BF16),
            pltpu.VMEM((2, 2, cut, hd), F32),
            pltpu.VMEM((2, 2, cut, hd), BF16),
            pltpu.VMEM((2, 2, half, hd), BF16),
            pltpu.VMEM((n_blocks, *shape), F32),
            pltpu.VMEM((2, n_z, *shape), F32),
            pltpu.VMEM((3, n_z // min(PARTS, n_z // 2), *shape), BF16),
            pltpu.VMEM((3, n_z // min(PARTS, n_z // 2), *shape), BF16),
            pltpu.VMEM((2, n_z, *shape), BF16),
            pltpu.VMEM((2, n_z, *shape), BF16),
            pltpu.VMEM((n_z, *shape), BF16),
            pltpu.VMEM((n_z, *shape), BF16),
            pltpu.VMEM((n_z, *shape), BF16),
            pltpu.VMEM((n_z - 1, *shape), BF16),
            dma((11,)),
            pltpu.SemaphoreType.REGULAR((4,)),
            dma((2, 6)),
            dma((2, 6)),
            dma((2, n_x - 1)),
            dma((2, n_x - 1)),
            dma((2, 5, n_y)),
            dma((2, 5, n_y)),
            dma((2, n_x - 1)),
            dma((2, n_x - 1)),
            dma((3,)),
            dma((3,)),
            dma((2, PARTS)),
            dma((2, PARTS)),
            dma((PARTS,)),
            dma((PARTS,)),
            dma((n_z - 1,)),
            dma((n_z - 1,)),
        ],
        compiler_params=pltpu.CompilerParams(
            collective_id=0, has_side_effects=True, vmem_limit_bytes=60 * 1024 * 1024
        ),
    )(block_order, owners, layer_input, query_heads, key_head, value_head, attn_grad)
    return pl.pallas_call(
        functools.partial(finish, 1.0 / math.sqrt(rows * n_seq)),
        out_shape=(query_part, stat, stat, stat),
        in_specs=[vmem, vmem],
        out_specs=(vmem, vmem, vmem, vmem),
        compiler_params=pltpu.CompilerParams(vmem_limit_bytes=60 * 1024 * 1024),
    )(query_grad, owned)


def solution(mesh):
    return jax.shard_map(
        functools.partial(shards, mesh.shape["seq"], mesh.shape["mp"]),
        mesh=mesh,
        in_specs=(
            P("seq", "mp"),
            P("seq", "mp"),
            P("seq", None),
            P("seq", None),
            P("seq", "mp"),
            P(),
            P("mp", None),
        ),
        out_specs=(
            P("seq", "mp"),
            P("mp", "seq", None, None),
            P("mp", "seq", None, None),
            P("mp", "seq", None, None),
        ),
        check_vma=False,
    )
```

time: 54.5 us -> 50.6 us (0.928)
  Pallas kernels: 53.7 us -> 49.8 us
    pallas_call x1, Pallas kernels: 51.9 us -> 48 us  [shards(): pl.pallas_call(functools.partial(kernel, n_seq, n_mp), out_shape=(query_p...]
where the time goes in v3:
time: 50.6 us; the launch traced here: 50.4 us
  Pallas kernels  49.8 us (98%)
  between operations  0.64 us (1%)
    pallas_call x1, Pallas kernels, shards(): pl.pallas_call(functools.partial(kernel, n_seq, n_mp), out_shape=(query_p...  48 us
    pallas_call x1, Pallas kernels, shards(): pl.pallas_call(functools.partial(finish, 1.0 / math.sqrt(rows * n_seq)),...  1.77 us

profile of v3, /device:TPU:1, one launch (start us, length us, event | category | flops | bytes accessed | tf_op | source)
XLA Modules:
  0.0 50.4 jit_solution(11897869168022056749)
XLA Ops:
  0.6 48.0 %shard_map.102 = (bf16[256,128]{1,0:T(8,128)(2,1)}, f32[32,128]{1,0:T(8,128)}) custom-call(s32[128]{0:T(128)} %order_hbm.1, s32[1,64]{1,0:T(1,128)} %owners_hbm.1, bf16[256,1024]{1,0:T(8,128)(2,1)} %x_hbm.1, bf16[256,128]{1,0:T(8,128)(2,1)} %q_hbm.1, bf16[256,128]{1,0:T(8,128)(2,1)} %k_hbm.1, bf16[256,128]{1,0:T(8,128)(2,1)} %v_hbm.1, bf16[256,128]{1,0:T(8,128)(2,1)} %g_hbm.1), custom_call_target="tpu_custom_call" | custom-call | tf_op jit(solution)/shard_map/pallas_call | solution.py:516
  48.7 1.8 %shard_map.103 = (bf16[256,128]{1,0:T(8,128)(2,1)}, f32[1,1,64,64]{3,2,1,0:T(8,128)}, f32[1,1,64,64]{3,2,1,0:T(8,128)}, f32[1,1,64,64]{3,2,1,0:T(8,128)}) custom-call(bf16[256,128]{1,0:T(8,128)(2,1)} %get-tuple-element.6.qg_ref, f32[32,128]{1,0:T(8,128)} %get-tuple-element.7.sum_ref), custom_call_target="tpu_custom_call" | custom-call | tf_op jit(solution)/shard_map/pallas_call | solution.py:585

commit v4 on v3

--- a/solution.py
+++ b/solution.py
@@ -217,13 +217,13 @@
     xt_v[...] = x_v[...].T
     inv_copy.wait()
 
-    row = lax.broadcasted_iota(jnp.int32, (half, half), 0)
-    col = lax.broadcasted_iota(jnp.int32, (half, half), 1)
+    key_row = lax.broadcasted_iota(jnp.int32, (half, half), 0)
+    query_col = lax.broadcasted_iota(jnp.int32, (half, half), 1)
     queries = [q_ref[slot * half : (slot + 1) * half, :] for slot in range(2)]
     grads = [g_ref[slot * half : (slot + 1) * half, :] for slot in range(2)]
     by_row = ((1,), (1,))
-    scores_own = [contract(queries[slot], k_own[slot], by_row) for slot in range(2)]
-    dprob_own = [contract(grads[slot], v_own[slot], by_row) for slot in range(2)]
+    scores_own = [contract(k_own[slot], queries[slot], by_row) for slot in range(2)]
+    dprob_own = [contract(v_own[slot], grads[slot], by_row) for slot in range(2)]
 
     def before(slot, own, near_far, other):
         if slot == 0:
@@ -239,11 +239,11 @@
             ]
         return jnp.concatenate(blocks, 0)
 
-    def send_terms(j, terms, terms_in):
+    def send_terms(j, these, terms, terms_in):
         copies = [
             remote(
-                terms.at[:, pl.ds(pl.multiple_of(lax.rem(mate(0, b), n_x) * cut, cut), cut), :],
-                terms_in.at[i],
+                terms.at[these, pl.ds(pl.multiple_of(lax.rem(mate(0, b), n_x) * cut, cut), cut), :],
+                terms_in.at[i, these],
                 rs_send.at[j, i],
                 rs_recv.at[j, i],
                 (s, mate(0, b)),
@@ -265,43 +265,44 @@
         position = first if slot == 0 else 2 * n_seq - 1 - first
         visible = jnp.concatenate(
             [
-                row - col >= 0,
+                query_col >= key_row,
                 jnp.broadcast_to(position >= 1, (half, half)),
-                (row - col < 0) & (position >= 2),
+                (query_col < key_row) & (position >= 2),
             ],
-            1,
+            0,
         )
         scores = jnp.concatenate(
-            [scores_own[slot], contract(queries[slot], windows[slot], by_row)], 1
+            [scores_own[slot], contract(windows[slot], queries[slot], by_row)], 0
         )
         scores = jnp.where(visible, scores * score_scale, MASKED)
-        top = jnp.max(scores, -1, keepdims=True)
+        top = jnp.max(scores, 0, keepdims=True)
         raw = jnp.exp(scores - top)
-        probs.append(raw * (1.0 / jnp.sum(raw, -1, keepdims=True)))
+        probs.append(raw * (1.0 / jnp.sum(raw, 0, keepdims=True)))
         probs_b.append(probs[slot].astype(BF16))
-        value_grad = contract(probs_b[slot], grads[slot], ((0,), (0,))).astype(BF16)
+        value_grad = contract(probs_b[slot], grads[slot], ((1,), (0,))).astype(BF16)
         terms_v[3 * slot : 3 * slot + 3] = value_grad.reshape(3, half, hd)
-    rs_v_copies = send_terms(0, terms_v, terms_v_in)
+    rs_v_copies = send_terms(0, pl.ds(0, 6), terms_v, terms_v_in)
 
     for copy in v_copies:
         copy.wait_recv()
     dscores = []
+    rs_k_copies = []
     for slot in range(2):
         values = before(slot, v_own, v_in, v_other)
-        dprob = jnp.concatenate([dprob_own[slot], contract(grads[slot], values, by_row)], 1)
-        delta = jnp.sum(probs_b[slot].astype(F32) * dprob, -1, keepdims=True)
+        dprob = jnp.concatenate([dprob_own[slot], contract(values, grads[slot], by_row)], 0)
+        delta = jnp.sum(probs_b[slot].astype(F32) * dprob, 0, keepdims=True)
         dscores.append((probs[slot] * (dprob - delta)).astype(BF16))
-        key_grad = contract(dscores[slot], queries[slot], ((0,), (0,))).astype(BF16)
+        key_grad = contract(dscores[slot], queries[slot], ((1,), (0,))).astype(BF16)
         terms_k[3 * slot : 3 * slot + 3] = key_grad.reshape(3, half, hd)
-    rs_k_copies = send_terms(1, terms_k, terms_k_in)
+        rs_k_copies.append(send_terms(1 + slot, pl.ds(3 * slot, 3), terms_k, terms_k_in))
 
     for i in range(1, min(2, len(rounds))):
         heard(i)
     for i in range(2, len(rounds)):
         tell(i)
     for slot in range(2):
-        query_grad = contract(dscores[slot][:, :half], k_own[slot], ((1,), (0,)))
-        query_grad += contract(dscores[slot][:, half:], windows[slot], ((1,), (0,)))
+        query_grad = contract(dscores[slot][:half], k_own[slot], ((0,), (0,)))
+        query_grad += contract(dscores[slot][half:], windows[slot], ((0,), (0,)))
         qg_ref[slot * half : (slot + 1) * half, :] = (query_grad * score_scale).astype(BF16)
     qg_copy = pltpu.make_async_copy(qg_ref, qg_hbm, load_sem.at[10])
     qg_copy.start()
@@ -311,7 +312,8 @@
     def head_sum(copies, terms, terms_in):
         total = terms[:, my_rows, :].astype(F32)
         for i in reversed(range(n_x - 1)):
-            copies[i].wait_recv()
+            for part in copies:
+                part[i].wait_recv()
             total = total + terms_in[i].astype(F32)
         return total
 
@@ -375,7 +377,7 @@
         started.extend(copies)
         return copies
 
-    total_v = head_sum(rs_v_copies, terms_v, terms_v_in)
+    total_v = head_sum([rs_v_copies], terms_v, terms_v_in)
     pass_v_copies = give_back(1, total_v)
     total_k = head_sum(rs_k_copies, terms_k, terms_k_in) * score_scale
     pass_k_copies = give_back(0, total_k)
@@ -563,8 +565,8 @@
             pltpu.SemaphoreType.REGULAR((4,)),
             dma((2, 6)),
             dma((2, 6)),
-            dma((2, n_x - 1)),
-            dma((2, n_x - 1)),
+            dma((3, n_x - 1)),
+            dma((3, n_x - 1)),
             dma((2, 5, n_y)),
             dma((2, 5, n_y)),
             dma((2, n_x - 1)),

time: 50.6 us -> 50.6 us (level)
  no operation moved by 1% of the time
where the time goes in v4:
time: 50.6 us; the launch traced here: 50.5 us
  Pallas kernels  49.8 us (98%)
  between operations  0.64 us (1%)
    pallas_call x1, Pallas kernels, shards(): pl.pallas_call(functools.partial(kernel, n_seq, n_mp), out_shape=(query_p...  48 us
    pallas_call x1, Pallas kernels, shards(): pl.pallas_call(functools.partial(finish, 1.0 / math.sqrt(rows * n_seq)),...  1.77 us

profile of v4, /device:TPU:1, one launch (start us, length us, event | category | flops | bytes accessed | tf_op | source)
XLA Modules:
  0.0 50.5 jit_solution(522017109342392461)
XLA Ops:
  0.6 48.0 %shard_map.102 = (bf16[256,128]{1,0:T(8,128)(2,1)}, f32[32,128]{1,0:T(8,128)}) custom-call(s32[128]{0:T(128)} %order_hbm.1, s32[1,64]{1,0:T(1,128)} %owners_hbm.1, bf16[256,1024]{1,0:T(8,128)(2,1)} %x_hbm.1, bf16[256,128]{1,0:T(8,128)(2,1)} %q_hbm.1, bf16[256,128]{1,0:T(8,128)(2,1)} %k_hbm.1, bf16[256,128]{1,0:T(8,128)(2,1)} %v_hbm.1, bf16[256,128]{1,0:T(8,128)(2,1)} %g_hbm.1), custom_call_target="tpu_custom_call" | custom-call | tf_op jit(solution)/shard_map/pallas_call | solution.py:518
  48.7 1.8 %shard_map.103 = (bf16[256,128]{1,0:T(8,128)(2,1)}, f32[1,1,64,64]{3,2,1,0:T(8,128)}, f32[1,1,64,64]{3,2,1,0:T(8,128)}, f32[1,1,64,64]{3,2,1,0:T(8,128)}) custom-call(bf16[256,128]{1,0:T(8,128)(2,1)} %get-tuple-element.6.qg_ref, f32[32,128]{1,0:T(8,128)} %get-tuple-element.7.sum_ref), custom_call_target="tpu_custom_call" | custom-call | tf_op jit(solution)/shard_map/pallas_call | solution.py:587

commit v5 on v4

--- a/solution.py
+++ b/solution.py
@@ -472,11 +472,13 @@
     qg_copy.wait()
     owned = ours[part - 1]
     for p in reversed(range(n_z - 1)):
+        if p == 0:
+            for copy in z_copies[1:]:
+                copy.wait_send()
         z_copies[p].wait_recv()
         owned = owned + z_in[p].astype(F32)
     sum_ref[...] = owned
-    for copy in z_copies:
-        copy.wait_send()
+    z_copies[0].wait_send()
 
 
 def finish(weight_scale, qg_ref, sum_ref, qg_out, block_out, left_out, right_out):

time: 50.6 us -> 50.6 us (level)
  no operation moved by 1% of the time
where the time goes in v5:
time: 50.6 us; the launch traced here: 50.5 us
  Pallas kernels  49.8 us (98%)
  between operations  0.64 us (1%)
    pallas_call x1, Pallas kernels, shards(): pl.pallas_call(functools.partial(kernel, n_seq, n_mp), out_shape=(query_p...  48 us
    pallas_call x1, Pallas kernels, shards(): pl.pallas_call(functools.partial(finish, 1.0 / math.sqrt(rows * n_seq)),...  1.77 us

profile of v5, /device:TPU:1, one launch (start us, length us, event | category | flops | bytes accessed | tf_op | source)
XLA Modules:
  0.0 50.5 jit_solution(7950104707642020744)
XLA Ops:
  0.6 48.0 %shard_map.102 = (bf16[256,128]{1,0:T(8,128)(2,1)}, f32[32,128]{1,0:T(8,128)}) custom-call(s32[128]{0:T(128)} %order_hbm.1, s32[1,64]{1,0:T(1,128)} %owners_hbm.1, bf16[256,1024]{1,0:T(8,128)(2,1)} %x_hbm.1, bf16[256,128]{1,0:T(8,128)(2,1)} %q_hbm.1, bf16[256,128]{1,0:T(8,128)(2,1)} %k_hbm.1, bf16[256,128]{1,0:T(8,128)(2,1)} %v_hbm.1, bf16[256,128]{1,0:T(8,128)(2,1)} %g_hbm.1), custom_call_target="tpu_custom_call" | custom-call | tf_op jit(solution)/shard_map/pallas_call | solution.py:520
  48.7 1.8 %shard_map.103 = (bf16[256,128]{1,0:T(8,128)(2,1)}, f32[1,1,64,64]{3,2,1,0:T(8,128)}, f32[1,1,64,64]{3,2,1,0:T(8,128)}, f32[1,1,64,64]{3,2,1,0:T(8,128)}) custom-call(bf16[256,128]{1,0:T(8,128)(2,1)} %get-tuple-element.6.qg_ref, f32[32,128]{1,0:T(8,128)} %get-tuple-element.7.sum_ref), custom_call_target="tpu_custom_call" | custom-call | tf_op jit(solution)/shard_map/pallas_call | solution.py:589
